TPU v7x, 128 devices: a whole 4x4x4 slice. The times are simulated.
128 devices in a mesh: slab: 16 (over z, y), sub: 8 (over x, core).
Axes of the slice: x: 4, y: 4, z: 4, core: 2. Of those that a mesh axis runs over, the one named last changes fastest.
Arguments:
- multipole: bfloat16 [456, 65536], P(None, ('slab', 'sub')), may hold values from -6 to 6
- send_list: int32 [128, 8, 128], P(('slab', 'sub')), may hold values from -1 to 511, as said below
- source_slot: int32 [64, 65536], P(None, ('slab', 'sub')), may hold values from -1 to 1535, as said below
- m2l_ops: bfloat16 [64, 456, 456], P('slab'), may hold values from -0.03125 to 0.03125
- l2l_ops: bfloat16 [8, 456, 456], replicated, may hold values from -0.25 to 0.25
- coarse_exp: bfloat16 [456, 128], P(None, 'sub'), may hold values from -6 to 6
Outputs:
- local_exp: bfloat16 [456, 65536], P(None, ('slab', 'sub'))
Inputs may be any that keep to these rules, and one draw needn't show every extreme that they name: send_list[o, n] holds, in its first slots, between 1 and 128 distinct positions of boxes on device o where the device in direction n exists, and -1 in all slots where it does not; in every draw some device fills all 128 slots toward each of its neighbours. source_slot[k, t] is -1 (no interaction), a position below 512 of a box on the target's own device, or 512 + n * 128 + j for a filled slot j of send_list[o, n] with o the target device's neighbour in the direction opposite to n.
All inputs are finite; a program needn't handle non-finite values.
Results may differ from a plain program's by a relative error of at most 0.0051.
Values may be sent and summed in bfloat16 or wider, within the bound.
A program may use at most 128 MiB of HBM per device.

v0:
```python
import jax
import jax.numpy as jnp
from jax import lax
from jax.sharding import PartitionSpec as P

DIR_SLAB = (-1, -1, -1, 0, 0, 1, 1, 1)
DIR_SUB = (-1, 0, 1, -1, 1, -1, 0, 1)


def from_behind(value, axis, by):
    peers = lax.axis_size(axis)
    pairs = [(i, i + by) for i in range(peers) if 0 <= i + by < peers]
    return lax.ppermute(value, axis, pairs)


def descend(operators, parents):
    children = jnp.einsum("ock,kp->cpo", operators, parents, preferred_element_type=jnp.float32)
    return children.reshape(parents.shape[0], -1)


def apply_offsets(running, weights, positions, row_table):
    row_count = row_table.shape[0]

    def one_offset(total, operand_pair):
        weight, position = operand_pair
        taken = jnp.take(row_table, jnp.clip(position, 0, row_count - 1), axis=0)
        taken = jnp.where((position >= 0)[:, None], taken, jnp.zeros((), taken.dtype))
        product = lax.dot_general(
            taken, weight, (((1,), (1,)), ((), ())), preferred_element_type=jnp.float32
        )
        return (total + product, None)

    result, _ = lax.scan(one_offset, running, (weights, positions))
    return result


def shards(multipole, send_list, source_slot, m2l_ops, l2l_ops, coarse_exp):
    sub_count = lax.axis_size("sub")
    coef_rows = multipole.shape[0]
    box_count = multipole.shape[1]
    slot_width = send_list.shape[2]
    outgoing = send_list[0]
    own_rows = multipole.T
    picked = jnp.take(own_rows, jnp.clip(outgoing.reshape(-1), 0, box_count - 1), axis=0)
    picked = picked.reshape(8, slot_width, coef_rows)
    picked = jnp.where((outgoing >= 0)[:, :, None], picked, jnp.zeros((), picked.dtype))
    arrived = [picked[direction] for direction in range(8)]
    for direction in range(8):
        arrived[direction] = from_behind(
            arrived[direction],
            ("slab", "sub"),
            DIR_SLAB[direction] * sub_count + DIR_SUB[direction],
        )
    ghost_rows = jnp.concatenate(arrived, axis=0)
    row_table = jnp.concatenate([own_rows, ghost_rows], axis=0)
    gathered, slot_all = (
        lax.all_gather(row_table.T, "slab", axis=1, tiled=True),
        lax.all_gather(source_slot, "slab", axis=1, tiled=True),
    )
    gathered_rows = gathered.T
    group_size = m2l_ops.shape[0]
    mine = lax.dynamic_slice_in_dim(slot_all, lax.axis_index("slab") * group_size, group_size, 0)
    block_base = jnp.arange(slot_all.shape[1], dtype=jnp.int32) // box_count * row_table.shape[0]
    positions = jnp.where(mine >= 0, mine + block_base[None, :], -1)
    partial_value = apply_offsets(
        jnp.zeros((slot_all.shape[1], coef_rows), jnp.float32), m2l_ops, positions, gathered_rows
    )
    far = lax.psum_scatter(partial_value.T, "slab", scatter_dimension=1, tiled=True)
    coarse_all = lax.all_gather(coarse_exp, "sub", axis=1, tiled=True)
    first_box = (lax.axis_index("slab") * sub_count + lax.axis_index("sub")) * box_count
    upper_count = max(box_count // 512, 1)
    ancestor = lax.dynamic_slice_in_dim(coarse_all, first_box // 512, upper_count, 1)
    level_one = descend(l2l_ops, ancestor).astype(jnp.bfloat16)
    level_two = descend(l2l_ops, level_one).astype(jnp.bfloat16)
    finest = descend(l2l_ops, level_two)
    return (far + finest).astype(jnp.bfloat16)


def solution(mesh):
    placed = (
        P(None, ("slab", "sub")),
        P(("slab", "sub"), None, None),
        P(None, ("slab", "sub")),
        P("slab", None, None),
        P(),
        P(None, "sub"),
    )
    return jax.shard_map(
        shards, mesh=mesh, in_specs=placed, out_specs=P(None, ("slab", "sub")), check_vma=False
    )
```

profile of v0, /device:TPU:1, one launch (start us, length us, event | category | flops | bytes accessed | tf_op | source)
XLA Modules:
  0.0 589.9 jit_solution(211348062754752508)
XLA Ops:
  6.5 0.0 all-gather.3.cloned.1.call-start
  6.5 0.7 all-gather.3.cloned.1.call-update
  7.3 0.0 all-gather.5.cloned.1.call-start
  7.3 1.2 copy.8
  8.5 0.7 broadcast_clamp_fusion.2
  9.2 0.0 copy-start.2
  9.3 4.0 gather_fusion.1
  13.2 0.0 copy-done.2
  13.3 0.5 select_select_fusion
  13.7 0.1 slice_bitcast_fusion
  13.8 1.3 collective-permute-start
  15.1 1.3 collective-permute-start.1
  16.4 1.3 collective-permute-start.2
  17.7 3.3 collective-permute-start.3
  21.1 3.1 collective-permute-start.4
  24.2 0.0 collective-permute-done
  24.2 5.4 collective-permute-start.5
  29.6 0.0 collective-permute-done.1
  29.6 4.5 collective-permute-start.6
  34.2 0.0 collective-permute-done.2
  34.2 5.1 collective-permute-start.7
  39.3 0.0 collective-permute-done.3
  39.4 0.0 collective-permute-done.4
  39.4 0.0 collective-permute-done.5
  39.4 0.0 collective-permute-done.6
  39.4 1.8 collective-permute-done.7
  41.2 0.0 copy-start.1
  41.3 1.2 copy-done.1
  42.4 0.0 all-gather.5.cloned.1.call-update
  42.5 0.0 reduce-scatter.2.cloned.1.call-start
  42.5 17.8 %all-gather.3.cloned.1.call-done = s32[64,8192]{1,0:T(8,128)} async-done(((s32[64,512]{1,0:T(8,128)}), s32[64,8192]{1,0:T(8,128)}) %all-gather.3.cloned.1.call-update) | async-done | bytes 2097168 | tf_op jit(solution)/shard_map/all_gather | solution.py:58
  60.3 1.0 add_select_fusion
  61.3 154.7 %all-gather.5.cloned.1.call-done = bf16[456,24576]{0,1:T(8,128)(2,1)} async-done(((bf16[456,1536]{0,1:T(8,128)(2,1)}), bf16[456,24576]{0,1:T(8,128)(2,1)}) %all-gather.5.cloned.1.call-update) | async-done | bytes 22413328 | tf_op jit(solution)/shard_map/all_gather | solution.py:57
  216.1 237.5 %while.11 = (s32[]{:T(128)}, f32[8192,456]{0,1:T(8,128)}, s32[4,8192]{1,0:T(4,128)S(1)}, bf16[24576,456]{1,0:T(8,128)(2,1)}, bf16[4,456,456]{2,1,0:T(8,128)(2,1)}, /*index=5*/s32[]{:T(128)}, s32[]{:T(128)}) while((s32[]{:T(128)}, f32[8192,456]{0,1:T(8,128)}, s32[4,8192]{1,0:T(4,128)S(1)}, bf16[24576,456]{1,0:T(8,128)(2,1)}, ...), condition=%wide.region_1.2_spmd.clone, body=%wide.region_0.1_spmd.clone.sunk | while | flops 3421863936 | bytes 53977192 | solution.py:33
  216.1 0.1 compare_select_fusion.5
  216.2 45.3 %gather_fusion = bf16[8192,456]{1,0:T(8,128)(2,1)} fusion(bf16[24576,456]{1,0:T(8,128)(2,1)} %get-tuple-element.123, s32[8192]{0:T(1024)S(1)} %broadcast_clamp_fusion.4), kind=kCustom, calls=%fused_computation.clone.clone.1 | custom fusion | bytes 14974976 | tf_op jit(solution)/shard_map/while/body/eval_jaxpr/jit(_take)/gather | solution.py:26
  261.5 0.1 compare_reduce_fusion.2
  261.6 11.4 %select_add_fusion.2 = f32[8192,456]{0,1:T(8,128)} fusion(f32[8192,456]{0,1:T(8,128)} %get-tuple-element.114, bf16[8192,456]{1,0:T(8,128)(2,1)} %gather_fusion, pred[8192]{0:T(1024)(128)(4,1)S(1)} %compare_and_fusion.3, pred[8192]{0:T(1024)(128)(4,1)S(1)} %compare_reduce_fusion.2, pred[]{:T(512)S(6)} %compare.9, ...), kind=kOutput, calls=%fused_computation.2.clone.1 | convolution fusion | flops 3421765632 | bytes 38756356 | tf_op jit(solution)/shard_map/while/body/eval_jaxpr/dot_general | solution.py:28
  273.1 0.1 compare_select_fusion.5
  273.2 45.3 %gather_fusion = bf16[8192,456]{1,0:T(8,128)(2,1)} fusion(bf16[24576,456]{1,0:T(8,128)(2,1)} %get-tuple-element.123, s32[8192]{0:T(1024)S(1)} %broadcast_clamp_fusion.4), kind=kCustom, calls=%fused_computation.clone.clone.1 | custom fusion | bytes 14974976 | tf_op jit(solution)/shard_map/while/body/eval_jaxpr/jit(_take)/gather | solution.py:26
  318.5 0.1 compare_reduce_fusion.2
  318.6 14.6 %select_add_fusion.2 = f32[8192,456]{0,1:T(8,128)} fusion(f32[8192,456]{0,1:T(8,128)} %get-tuple-element.114, bf16[8192,456]{1,0:T(8,128)(2,1)} %gather_fusion, pred[8192]{0:T(1024)(128)(4,1)S(1)} %compare_and_fusion.3, pred[8192]{0:T(1024)(128)(4,1)S(1)} %compare_reduce_fusion.2, pred[]{:T(512)S(6)} %compare.9, ...), kind=kOutput, calls=%fused_computation.2.clone.1 | convolution fusion | flops 3421765632 | bytes 38756356 | tf_op jit(solution)/shard_map/while/body/eval_jaxpr/dot_general | solution.py:28
  333.2 0.1 compare_select_fusion.5
  333.3 45.3 %gather_fusion = bf16[8192,456]{1,0:T(8,128)(2,1)} fusion(bf16[24576,456]{1,0:T(8,128)(2,1)} %get-tuple-element.123, s32[8192]{0:T(1024)S(1)} %broadcast_clamp_fusion.4), kind=kCustom, calls=%fused_computation.clone.clone.1 | custom fusion | bytes 14974976 | tf_op jit(solution)/shard_map/while/body/eval_jaxpr/jit(_take)/gather | solution.py:26
  378.6 0.1 compare_reduce_fusion.2
  378.8 14.7 %select_add_fusion.2 = f32[8192,456]{0,1:T(8,128)} fusion(f32[8192,456]{0,1:T(8,128)} %get-tuple-element.114, bf16[8192,456]{1,0:T(8,128)(2,1)} %gather_fusion, pred[8192]{0:T(1024)(128)(4,1)S(1)} %compare_and_fusion.3, pred[8192]{0:T(1024)(128)(4,1)S(1)} %compare_reduce_fusion.2, pred[]{:T(512)S(6)} %compare.9, ...), kind=kOutput, calls=%fused_computation.2.clone.1 | convolution fusion | flops 3421765632 | bytes 38756356 | tf_op jit(solution)/shard_map/while/body/eval_jaxpr/dot_general | solution.py:28
  393.5 0.1 compare_select_fusion.5
  393.6 45.3 %gather_fusion = bf16[8192,456]{1,0:T(8,128)(2,1)} fusion(bf16[24576,456]{1,0:T(8,128)(2,1)} %get-tuple-element.123, s32[8192]{0:T(1024)S(1)} %broadcast_clamp_fusion.4), kind=kCustom, calls=%fused_computation.clone.clone.1 | custom fusion | bytes 14974976 | tf_op jit(solution)/shard_map/while/body/eval_jaxpr/jit(_take)/gather | solution.py:26
  438.9 0.1 compare_reduce_fusion.2
  439.0 14.6 %select_add_fusion.2 = f32[8192,456]{0,1:T(8,128)} fusion(f32[8192,456]{0,1:T(8,128)} %get-tuple-element.114, bf16[8192,456]{1,0:T(8,128)(2,1)} %gather_fusion, pred[8192]{0:T(1024)(128)(4,1)S(1)} %compare_and_fusion.3, pred[8192]{0:T(1024)(128)(4,1)S(1)} %compare_reduce_fusion.2, pred[]{:T(512)S(6)} %compare.9, ...), kind=kOutput, calls=%fused_computation.2.clone.1 | convolution fusion | flops 3421765632 | bytes 38756356 | tf_op jit(solution)/shard_map/while/body/eval_jaxpr/dot_general | solution.py:28
  453.6 16.7 %copy.9 = f32[8192,456]{1,0:T(8,128)} copy(f32[8192,456]{0,1:T(8,128)} %get-tuple-element.32) | data formatting | bytes 29884416 | tf_op jit(solution)/shard_map/while | solution.py:33
  470.3 0.0 copy-start.3
  470.3 0.0 reduce-scatter.2.cloned.1.call-update
  470.4 0.7 copy-done.3
  471.0 0.0 copy-start
  471.0 13.7 %all_gather.11 = bf16[456,128]{0,1:T(8,128)(2,1)S(1)} all-gather(bf16[456,16]{0,1:T(8,128)(2,1)S(1)} %copy-done.3), channel_id=1, replica_groups=mesh['slab'=16,'sub'=8] {'sub'}, dimensions={1}, use_global_device_ids=true | all-gather | bytes 131328 | tf_op jit(solution)/shard_map/all_gather | solution.py:69
  484.7 3.2 fusion.21
  487.9 0.0 copy-done
  487.9 1.1 fusion.11
  489.0 1.2 convolution_bitcast_fusion
  490.2 90.3 %reduce-scatter.2.cloned.1.call-done = f32[456,512]{0,1:T(8,128)} async-done(((f32[456,8192]{0,1:T(8,128)}), f32[456,512]{0,1:T(8,128)}) %reduce-scatter.2.cloned.1.call-update) | async-done | bytes 933904 | tf_op jit(solution)/shard_map/reduce_scatter | solution.py:68
  580.5 1.8 fusion.12
  582.4 1.0 copy.12
  (23 shorter events, 0.3 us)
Async XLA Ops:
  6.5 53.8 %all-gather.3.cloned.1.call-start = ((), (), s32[]{:S(2)}) async-start(), calls=%async_computation.1 | async-start | bytes 2228224 | tf_op jit(solution)/shard_map/all_gather | solution.py:58
  7.3 208.8 %all-gather.5.cloned.1.call-start = ((), (), s32[]{:S(2)}) async-start(), calls=%async_computation.2 | async-start | bytes 26738688 | tf_op jit(solution)/shard_map/all_gather | solution.py:57
  9.2 4.0 copy-start.2
  13.8 10.4 %collective-permute-start = (bf16[128,456]{1,0:T(8,128)(2,1)S(1)}, bf16[128,456]{1,0:T(8,128)(2,1)S(1)}, u32[]{:S(2)}, u32[]{:S(2)}) collective-permute-start(bf16[128,456]{1,0:T(8,128)(2,1)S(1)} %get-tuple-element.70), channel_id=1, source_target_pairs={{9,0},{10,1},{11,2},{12,3},{13,4},{14,5},{15,6},{16,7},{17,8},{18,... | collective-permute-start | bytes 350216 | tf_op jit(solution)/shard_map/ppermute | solution.py:13
  15.1 14.5 %collective-permute-start.1 = (bf16[128,456]{1,0:T(8,128)(2,1)S(1)}, bf16[128,456]{1,0:T(8,128)(2,1)S(1)}, u32[]{:S(2)}, u32[]{:S(2)}) collective-permute-start(bf16[128,456]{1,0:T(8,128)(2,1)S(1)} %get-tuple-element.69), channel_id=1, source_target_pairs={{8,0},{9,1},{10,2},{11,3},{12,4},{13,5},{14,6},{15,7},{16,8},{17,9... | collective-permute-start | bytes 350216 | tf_op jit(solution)/shard_map/ppermute | solution.py:13
  16.4 17.8 %collective-permute-start.2 = (bf16[128,456]{1,0:T(8,128)(2,1)S(1)}, bf16[128,456]{1,0:T(8,128)(2,1)S(1)}, u32[]{:S(2)}, u32[]{:S(2)}) collective-permute-start(bf16[128,456]{1,0:T(8,128)(2,1)S(1)} %get-tuple-element.68), channel_id=1, source_target_pairs={{7,0},{8,1},{9,2},{10,3},{11,4},{12,5},{13,6},{14,7},{15,8},{16,9}... | collective-permute-start | bytes 350216 | tf_op jit(solution)/shard_map/ppermute | solution.py:13
  17.7 21.6 %collective-permute-start.3 = (bf16[128,456]{1,0:T(8,128)(2,1)S(1)}, bf16[128,456]{1,0:T(8,128)(2,1)S(1)}, u32[]{:S(2)}, u32[]{:S(2)}) collective-permute-start(bf16[128,456]{1,0:T(8,128)(2,1)S(1)} %get-tuple-element.67), channel_id=1, source_target_pairs={{1,0},{2,1},{3,2},{4,3},{5,4},{6,5},{7,6},{8,7},{9,8},{10,9},{11,1... | collective-permute-start | bytes 350216 | tf_op jit(solution)/shard_map/ppermute | solution.py:13
  21.1 18.3 %collective-permute-start.4 = (bf16[128,456]{1,0:T(8,128)(2,1)S(1)}, bf16[128,456]{1,0:T(8,128)(2,1)S(1)}, u32[]{:S(2)}, u32[]{:S(2)}) collective-permute-start(bf16[128,456]{1,0:T(8,128)(2,1)S(1)} %get-tuple-element.66), channel_id=1, source_target_pairs={{0,1},{1,2},{2,3},{3,4},{4,5},{5,6},{6,7},{7,8},{8,9},{9,10},{10,1... | collective-permute-start | bytes 350216 | tf_op jit(solution)/shard_map/ppermute | solution.py:13
  24.2 15.2 %collective-permute-start.5 = (bf16[128,456]{1,0:T(8,128)(2,1)S(1)}, bf16[128,456]{1,0:T(8,128)(2,1)S(1)}, u32[]{:S(2)}, u32[]{:S(2)}) collective-permute-start(bf16[128,456]{1,0:T(8,128)(2,1)S(1)} %get-tuple-element.65), channel_id=1, source_target_pairs={{0,7},{1,8},{2,9},{3,10},{4,11},{5,12},{6,13},{7,14},{8,15},{9,16}... | collective-permute-start | bytes 350216 | tf_op jit(solution)/shard_map/ppermute | solution.py:13
  29.6 9.8 %collective-permute-start.6 = (bf16[128,456]{1,0:T(8,128)(2,1)S(1)}, bf16[128,456]{1,0:T(8,128)(2,1)S(1)}, u32[]{:S(2)}, u32[]{:S(2)}) collective-permute-start(bf16[128,456]{1,0:T(8,128)(2,1)S(1)} %get-tuple-element.64), channel_id=1, source_target_pairs={{0,8},{1,9},{2,10},{3,11},{4,12},{5,13},{6,14},{7,15},{8,16},{9,17... | collective-permute-start | bytes 350216 | tf_op jit(solution)/shard_map/ppermute | solution.py:13
  34.2 7.0 %collective-permute-start.7 = (bf16[128,456]{1,0:T(8,128)(2,1)S(1)}, bf16[128,456]{1,0:T(8,128)(2,1)S(1)}, u32[]{:S(2)}, u32[]{:S(2)}) collective-permute-start(bf16[128,456]{1,0:T(8,128)(2,1)S(1)} %get-tuple-element.63), channel_id=1, source_target_pairs={{0,9},{1,10},{2,11},{3,12},{4,13},{5,14},{6,15},{7,16},{8,17},{9,1... | collective-permute-start | bytes 350216 | tf_op jit(solution)/shard_map/ppermute | solution.py:13
  41.2 1.2 copy-start.1
  42.5 538.1 %reduce-scatter.2.cloned.1.call-start = ((), (), s32[]{:S(2)}) async-start(), calls=%async_computation.3 | async-start | bytes 17825792 | tf_op jit(solution)/shard_map/reduce_scatter | solution.py:68
  470.3 0.7 copy-start.3
  471.0 16.9 %copy-start = (bf16[8,456,456]{2,1,0:T(8,128)(2,1)S(1)}, bf16[8,456,456]{2,1,0:T(8,128)(2,1)}, u32[]{:S(2)}) copy-start(bf16[8,456,456]{2,1,0:T(8,128)(2,1)} %param.12) | copy-start | bytes 9980932
Sparse Core Ops, SparseCore 0:
  9.5 50.7 all-gather.2
  62.5 153.5 all-gather.4
  470.5 110.0 reduce-scatter.1
where the time goes:
time: 591 us; the launch traced here: 590 us
  waiting for transfers between devices  265 us (45%)
  local copies, waits for them, and re-layouts  206 us (35%)
  matrix products  60.8 us (10%)
  starting transfers between devices  25.4 us (4%)
  blocking collectives  13.7 us (2%)
  between operations  13.4 us (2%)
    gather x4, local copies, waits for them, and re-layouts, one_offset(): taken = jnp.take(row_table, jnp.clip(position, 0, row_count - 1), axis=0)  181 us
    all_gather x1, waiting for transfers between devices, shards(): lax.all_gather(row_table.T, 'slab', axis=1, tiled=True)  155 us
    reduce_scatter x1, waiting for transfers between devices, shards(): lax.psum_scatter(partial_value.T, 'slab', scatter_dimension=1, tiled=True)  90.3 us
    dot_general x4, matrix products, one_offset(): lax.dot_general(taken, weight, (((1,), (1,)), ((), ())), preferred_elemen...  55.3 us
    ppermute x8, starting transfers between devices, from_behind(): return lax.ppermute(value, axis, pairs)  25.3 us
    all_gather x1, waiting for transfers between devices, shards(): lax.all_gather(source_slot, 'slab', axis=1, tiled=True)  17.8 us
    while x1, local copies, waits for them, and re-layouts, apply_offsets(): result, _ = lax.scan(one_offset, running, (weights, positions))  16.7 us
    all_gather x1, blocking collectives, shards(): coarse_all = lax.all_gather(coarse_exp, 'sub', axis=1, tiled=True)  13.7 us
  transfers between devices with their start and end apart: 11, of which 4 were waited for; matrix products, arithmetic and copies ran while one was open for 2% of the time, Pallas kernels for 0%

commit v1 on v0

v1 whole, which is shorter than its diff:
```python
import jax
import jax.numpy as jnp
from jax import lax
from jax.experimental import pallas as pl
from jax.experimental.pallas import tpu as pltpu
from jax.sharding import PartitionSpec as P

DIR_SLAB = (-1, -1, -1, 0, 0, 1, 1, 1)
DIR_SUB = (-1, 0, 1, -1, 1, -1, 0, 1)
COEF, BOX, OFFSETS, CAP, COLS = 456, 512, 64, 128, 1536
LANES = 512
NT = (((1,), (1,)), ((), ()))
MESH = pl.DeviceIdType.MESH
AHEAD = 3
LATE = 1


def pick_rows(index_of, table_ref, picked_ref, unroll):
    def chunk(i, carry):
        for u in range(64):
            place = pl.multiple_of(i * 256 + (u // 8) * 32, 32) + u % 8
            picked_ref[pl.ds(place, 4, stride=8), :] = table_ref[index_of(i * 64 + u)]
        return carry
    lax.fori_loop(0, BOX // 64, chunk, 0, unroll=unroll)


def spread_rows(picked_ref, table_ref, first):
    def chunk(i, carry):
        for u in range(64):
            place = pl.multiple_of(i * 256 + (u // 8) * 32, 32) + u % 8
            table_ref[first + i * 64 + u] = picked_ref[pl.ds(place, 4, stride=8), :]
        return carry
    lax.fori_loop(0, BOX // 64, chunk, 0)


def picked_value(picked_ref):
    tiles = picked_ref[...].reshape(BOX // 8, 4, 8, 128)
    return jnp.concatenate(
        [tiles[:, c].reshape(BOX, 128) for c in range(4)], axis=1
    ).astype(jnp.bfloat16)


def set_picked(picked_ref, rows):
    tiles = [rows[:, c * 128 : (c + 1) * 128].reshape(BOX // 8, 8, 128) for c in range(4)]
    picked_ref[...] = jnp.stack(tiles, axis=1).reshape(BOX * 4, 128)


def pad_lanes(rows):
    return jnp.concatenate([rows, jnp.zeros((rows.shape[0], LANES - COEF), rows.dtype)], axis=1)


def kernel(
    multipole_ref, send_list_ref, slot_hbm, ops_hbm, l2l_hbm, coarse_ref, out_ref,
    slot_ref, ops_ref, l2l_ref, table_ref, even_ref, odd_ref, acc_ref, ghost_out, ghost_in,
    coarse_out, coarse_in, level_one, level_two,
    local_sem, op_send, op_recv, ghost_send, ghost_recv, coarse_send, coarse_recv,
):
    a, b = lax.axis_index("slab"), lax.axis_index("sub")
    z, y, x, core = a // 4, a % 4, b // 2, b % 2

    local = [
        pltpu.make_async_copy(slot_hbm, slot_ref, local_sem.at[0]),
        pltpu.make_async_copy(l2l_hbm, l2l_ref, local_sem.at[1]),
        pltpu.make_async_copy(ops_hbm, ops_ref.at[pl.ds(4 * a, 4)], local_sem.at[2]),
    ]
    for copy in local:
        copy.start()

    def exists(da, db):
        row, col = a + da, b + db
        return (row >= 0) & (row < 16) & (col >= 0) & (col < 8)

    ghost_in[...] = jnp.zeros_like(ghost_in)
    barrier = pltpu.get_barrier_semaphore()
    for step in range(1, 8):
        pl.semaphore_signal(barrier, inc=1, device_id=(a, (b + step) % 8), device_id_type=MESH)
    for dy, dz in ((1, 0), (3, 0), (0, 1), (0, 3)):
        there = ((z + dz) % 4) * 4 + (y + dy) % 4
        pl.semaphore_signal(barrier, inc=1, device_id=(there, b), device_id_type=MESH)
    greeted = 11
    for da, db in zip(DIR_SLAB, DIR_SUB):
        if da != 0:
            here = exists(da, db)

            @pl.when(here)
            def _():
                pl.semaphore_signal(barrier, inc=1, device_id=(a + da, b + db), device_id_type=MESH)

            greeted = greeted + here.astype(jnp.int32)

    own = jnp.concatenate(
        [multipole_ref[...].astype(jnp.float32), jnp.zeros((LANES - COEF, BOX), jnp.float32)], axis=0
    ).T
    set_picked(even_ref, own)
    table_ref[0] = jnp.zeros((4, 128), jnp.float32)
    spread_rows(even_ref, table_ref, 1)
    coarse = jnp.concatenate(
        [coarse_ref[...].astype(jnp.float32), jnp.zeros((LANES - COEF, 128), jnp.float32)], axis=0
    ).T
    coarse_out[...] = coarse[:16]

    pl.semaphore_wait(barrier, greeted)

    def source(cls, carrier, q1, q2):
        sign = 1 - 2 * carrier
        first = (q1 + (q1 == 2).astype(jnp.int32) - (q1 == 3).astype(jnp.int32)) * sign
        second = (q2 + (q2 == 2).astype(jnp.int32) - (q2 == 3).astype(jnp.int32)) * sign
        y0 = (y - jnp.where(cls == 0, first, second) + 4) % 4
        z0 = (z - jnp.where(cls == 0, second, first) + 4) % 4
        return y0, z0, 4 * (4 * z0 + y0) + 2 * carrier + cls

    sign = 1 - 2 * core

    def links(cls, q1, q2, own_op):
        y0, z0, k = source(cls, core, q1, q2)
        half = (x + y0 + z0 + cls) % 2 == 0
        number = k // 4 * 2 + cls
        src = ops_hbm.at[2 * core + cls] if own_op else ops_ref.at[k]

        def copy(kind, device):
            return pltpu.make_async_remote_copy(
                src_ref=src, dst_ref=ops_ref.at[k], send_sem=op_send.at[kind, number],
                recv_sem=op_recv.at[k], device_id=device, device_id_type=MESH,
            )

        def along(axis_is_y, by):
            ny = jnp.where(axis_is_y, (y + by + 4) % 4, y)
            nz = jnp.where(axis_is_y, z, (z + by + 4) % 4)
            return (4 * nz + ny, b)

        prim_y = cls == 0
        back = along(~prim_y, -sign)
        beside = (a, ((x + sign + 4) % 4) * 2 + core)
        kinds = [
            ((q2 == 0) & (q1 <= 1), lambda: copy(0, along(prim_y, sign))),
            ((q2 == 0) & (q1 == 0), lambda: copy(1, along(prim_y, -sign))),
            ((q2 == 0) | ((q2 == 1) & half), lambda: copy(2, along(~prim_y, sign))),
            (
                ((q2 == 0) | (q2 >= 2)) & half,
                lambda: copy(3, (jnp.where(q2 == 0, back[0], a), jnp.where(q2 == 0, b, beside[1]))),
            ),
            (q1 + q2 > 0, lambda: copy(4, (a, b + sign))),
        ]
        return k, kinds

    zero = jnp.int32(0)

    def start_own(cls, kinds):
        _, found = links(jnp.int32(cls), zero, zero, True)
        for kind in kinds:
            @pl.when(found[kind][0])
            def _():
                found[kind][1]().start()

    def over_x(cls, step):
        y0, z0, _ = source(cls, core, step % 4, step // 4)
        return (step >= 8) & ((x + y0 + z0 + cls) % 2 == 1)

    def forward(cls, step):
        k, found = links(cls, step % 4, step // 4, False)
        pltpu.make_async_copy(ops_ref.at[k], ops_ref.at[k], op_recv.at[k]).wait()
        for condition, copy in found:
            @pl.when(condition)
            def _():
                copy().start()

    start_own(0, (0, 1))
    start_own(1, (0, 1))

    has_coarse = b == a // 2

    def coarse_copy(step):
        return pltpu.make_async_remote_copy(
            src_ref=coarse_out.at[pl.ds(pl.multiple_of(a % 2 * 8, 8), 8)], dst_ref=coarse_in,
            send_sem=coarse_send.at[step - 1], recv_sem=coarse_recv,
            device_id=(a, (b + step) % 8), device_id_type=MESH,
        )

    @pl.when(has_coarse)
    def _():
        for step in range(1, 8):
            coarse_copy(step).start()
        coarse_in[...] = coarse_out[pl.ds(pl.multiple_of(a % 2 * 8, 8), 8), :]

    def ghost_copy(n):
        da, db = DIR_SLAB[n], DIR_SUB[n]
        return pltpu.make_async_remote_copy(
            src_ref=ghost_out.at[n], dst_ref=ghost_in.at[n], send_sem=ghost_send.at[n],
            recv_sem=ghost_recv.at[n], device_id=(a + da, b + db), device_id_type=MESH,
        )

    for part in range(2):
        pick_rows(
            lambda t: jnp.maximum(send_list_ref[0, 4 * part + t // CAP, t % CAP], 0) + 1,
            table_ref, odd_ref, False,
        )
        ghost_out[4 * part : 4 * part + 4] = picked_value(odd_ref).reshape(4, CAP, LANES)
        for n in range(4 * part, 4 * part + 4):
            @pl.when(exists(DIR_SLAB[n], DIR_SUB[n]))
            def _():
                ghost_copy(n).start()

    start_own(0, (2, 3))
    start_own(1, (2, 3))

    @pl.when(jnp.logical_not(has_coarse))
    def _():
        coarse_copy(1).wait_recv()
    local[1].wait()

    parent = jnp.broadcast_to(coarse_in[pl.ds(b, 1), :], (8, LANES))[:, :COEF].astype(jnp.bfloat16)
    for o in range(8):
        child = lax.dot_general(parent, l2l_ref[o], NT, preferred_element_type=jnp.float32)
        level_one[o : o + 1, :] = pad_lanes(child)[:1]
    parents = level_one[...][:, :COEF].astype(jnp.bfloat16)
    for o in range(8):
        children = pad_lanes(lax.dot_general(parents, l2l_ref[o], NT, preferred_element_type=jnp.float32))
        for c in range(4):
            level_two[c, pl.ds(o, 8, stride=8), :] = children[:, c * 128 : (c + 1) * 128]

    def apply(weight, picked_ref):
        acc_ref[...] += lax.dot_general(
            weight, picked_value(picked_ref)[:, :COEF], NT, preferred_element_type=jnp.float32
        )

    acc_ref[...] = jnp.zeros_like(acc_ref)
    even_ref[...] = jnp.zeros_like(even_ref)

    def octant(o, carry):
        for c in range(4):
            rounded = level_two[c].astype(jnp.bfloat16).astype(jnp.float32)
            even_ref[pl.ds(c * 8 + o, BOX // 8, stride=32), :] = rounded
        apply(l2l_ref[o], even_ref)
        for c in range(4):
            even_ref[pl.ds(c * 8 + o, BOX // 8, stride=32), :] = jnp.zeros((BOX // 8, 128), jnp.float32)
        return carry

    lax.fori_loop(0, 8, octant, 0)

    for part in range(2):
        for n in range(4 * part, 4 * part + 4):
            @pl.when(exists(-DIR_SLAB[n], -DIR_SUB[n]))
            def _():
                ghost_copy(n).wait_recv()
        set_picked(odd_ref, ghost_in[4 * part : 4 * part + 4].reshape(BOX, LANES).astype(jnp.float32))
        spread_rows(odd_ref, table_ref, 1 + BOX + part * BOX)

    local[0].wait()
    local[2].wait()
    for step in range(1, AHEAD):
        forward(jnp.int32(0), jnp.int32(step))
        forward(jnp.int32(1), jnp.int32(step))

    def op_pair(i):
        step, carrier = i // 2, (core + i) % 2
        return (
            source(jnp.int32(0), carrier, step % 4, step // 4)[2],
            source(jnp.int32(1), carrier, step % 4, step // 4)[2],
        )

    def pick(k, picked_ref, unroll=True):
        pick_rows(lambda t: slot_ref[k, t] + 1, table_ref, picked_ref, unroll)

    pick(op_pair(jnp.int32(0))[0], even_ref, False)

    def main(i, carry):
        early, late = i // 2 + AHEAD, i // 2 + LATE

        @pl.when((early < 16) & jnp.logical_not(over_x(i % 2, early)))
        def _():
            forward(i % 2, early)

        @pl.when((late < 16) & over_x(i % 2, late))
        def _():
            forward(i % 2, late)

        k_even, k_odd = op_pair(i)
        k_next = op_pair(jnp.minimum(i + 1, 31))[0]

        @pl.when((i % 2 == 1) & (i > 1))
        def _():
            for k in (k_even, k_odd):
                pltpu.make_async_copy(ops_ref.at[k], ops_ref.at[k], op_recv.at[k]).wait()

        pick(k_odd, odd_ref)
        apply(ops_ref[k_even], even_ref)
        pick(k_next, even_ref)
        apply(ops_ref[k_odd], odd_ref)
        return carry

    lax.fori_loop(0, 32, main, 0)
    out_ref[...] = acc_ref[...].astype(out_ref.dtype)

    for cls in (0, 1):
        _, found = links(jnp.int32(cls), zero, zero, True)
        for kind in range(4):
            @pl.when(found[kind][0])
            def _():
                found[kind][1]().wait_send()

    def drain(i, carry):
        step = i // 2
        _, found = links(i % 2, step % 4, step // 4, False)
        for condition, copy in found:
            @pl.when(condition)
            def _():
                copy().wait_send()
        return carry

    lax.fori_loop(2, 32, drain, 0)
    for n in range(8):
        @pl.when(exists(DIR_SLAB[n], DIR_SUB[n]))
        def _():
            ghost_copy(n).wait_send()

    @pl.when(has_coarse)
    def _():
        for step in range(1, 8):
            coarse_copy(step).wait_send()


def shards(multipole, send_list, source_slot, m2l_ops, l2l_ops, coarse_exp):
    coarse = jnp.pad(coarse_exp, ((0, 0), (0, 112)))
    vmem = pl.BlockSpec(memory_space=pltpu.VMEM)
    smem = pl.BlockSpec(memory_space=pltpu.SMEM)
    hbm = pl.BlockSpec(memory_space=pltpu.HBM)
    f32, bf16 = jnp.float32, jnp.bfloat16
    return pl.pallas_call(
        kernel,
        out_shape=jax.ShapeDtypeStruct((COEF, BOX), bf16),
        in_specs=[vmem, smem, hbm, hbm, hbm, vmem],
        out_specs=vmem,
        scratch_shapes=[
            pltpu.SMEM((OFFSETS, BOX), jnp.int32),
            pltpu.VMEM((OFFSETS, COEF, COEF), bf16),
            pltpu.VMEM((8, COEF, COEF), bf16),
            pltpu.VMEM((COLS + 8, 4, 128), f32),
            pltpu.VMEM((BOX * 4, 128), f32),
            pltpu.VMEM((BOX * 4, 128), f32),
            pltpu.VMEM((COEF, BOX), f32),
            pltpu.VMEM((8, CAP, LANES), bf16),
            pltpu.VMEM((8, CAP, LANES), bf16),
            pltpu.VMEM((16, LANES), f32),
            pltpu.VMEM((8, LANES), f32),
            pltpu.VMEM((8, LANES), f32),
            pltpu.VMEM((4, 64, 128), f32),
            pltpu.SemaphoreType.DMA((3,)),
            pltpu.SemaphoreType.DMA((5, 32)),
            pltpu.SemaphoreType.DMA((OFFSETS,)),
            pltpu.SemaphoreType.DMA((8,)),
            pltpu.SemaphoreType.DMA((8,)),
            pltpu.SemaphoreType.DMA((7,)),
            pltpu.SemaphoreType.DMA,
        ],
        compiler_params=pltpu.CompilerParams(
            collective_id=0, has_side_effects=True, vmem_limit_bytes=60 * 2**20
        ),
        name="translate",
    )(multipole, send_list, source_slot, m2l_ops, l2l_ops, coarse)


def solution(mesh):
    placed = (
        P(None, ("slab", "sub")),
        P(("slab", "sub"), None, None),
        P(None, ("slab", "sub")),
        P("slab", None, None),
        P(),
        P(None, "sub"),
    )
    return jax.shard_map(
        shards, mesh=mesh, in_specs=placed, out_specs=P(None, ("slab", "sub")), check_vma=False
    )
```

time: 591 us -> 129 us (0.22)
  waiting for transfers between devices: 265 us -> 0 us
  local copies, waits for them, and re-layouts: 206 us -> 3.35 us
  Pallas kernels: 0 us -> 124 us
  matrix products: 60.8 us -> 0 us
  starting transfers between devices: 25.4 us -> 0 us
  blocking collectives: 13.7 us -> 0 us
  between operations: 13.4 us -> 0.01 us
    gather x5 -> x0, local copies, waits for them, and re-layouts: 185 us -> none  [the longest x4 181 us: one_offset(): taken = jnp.take(row_table, jnp.clip(position, 0, row_count - 1), axis=0)]
    all_gather x2 -> x0, waiting for transfers between devices: 173 us -> none  [the longest x1 155 us: shards(): lax.all_gather(row_table.T, 'slab', axis=1, tiled=True)]
    pallas_call x0 -> x1, Pallas kernels: none -> 124 us  [shards(): pl.pallas_call(kernel, out_shape=jax.ShapeDtypeStruct((COEF, BOX), bf16),...]
    reduce_scatter x1 -> x0, waiting for transfers between devices: 90.3 us -> none  [shards(): lax.psum_scatter(partial_value.T, 'slab', scatter_dimension=1, tiled=True)]
    dot_general x7 -> x0, matrix products: 60.8 us -> none  [the longest x4 55.3 us: one_offset(): lax.dot_general(taken, weight, (((1,), (1,)), ((), ())), preferred_elemen...]
    ppermute x8 -> x0, starting transfers between devices: 25.3 us -> none  [from_behind(): return lax.ppermute(value, axis, pairs)]
    while x1 -> x0, local copies, waits for them, and re-layouts: 16.7 us -> none  [apply_offsets(): result, _ = lax.scan(one_offset, running, (weights, positions))]
    all_gather x1 -> x0, blocking collectives: 13.7 us -> none  [shards(): coarse_all = lax.all_gather(coarse_exp, 'sub', axis=1, tiled=True)]
  transfers between devices with their start and end apart: 11 -> 0, of which waited for: 4 -> 0; matrix products, arithmetic and copies ran while one was open for 2% -> 0% of each run, Pallas kernels for 0% -> 0%
where the time goes in v1:
time: 129 us; the launch traced here: 127 us
  Pallas kernels  124 us (96%)
  local copies, waits for them, and re-layouts  3.35 us (3%)
    pallas_call x1, Pallas kernels, shards(): pl.pallas_call(kernel, out_shape=jax.ShapeDtypeStruct((COEF, BOX), bf16),...  124 us
    unnamed x2, local copies, waits for them, and re-layouts  2.68 us

profile of v1, /device:TPU:1, one launch (start us, length us, event | category | flops | bytes accessed | tf_op | source)
XLA Modules:
  0.0 127.2 jit_solution(14605885740300892595)
XLA Ops:
  0.0 0.9 copy.7
  0.9 0.7 pad.4.coarse_ref
  1.5 123.8 %translate.1 = bf16[456,512]{1,0:T(8,128)(2,1)} custom-call(bf16[456,512]{1,0:T(8,128)(2,1)} %multipole_ref.1, s32[1,8,128]{2,1,0:T(8,128)} %send_list_ref.1, s32[64,512]{1,0:T(8,128)} %slot_hbm.1, bf16[4,456,456]{2,1,0:T(8,128)(2,1)} %ops_hbm.1, bf16[8,456,456]{2,1,0:T(8,128)(2,1)} %l2l_hbm.1, bf16[456,128]{1,0:T(8,128)(2,1)} %pad.4.coarse_ref), custom_call_target="tpu_custom_call" | custom-call | tf_op jit(solution)/shard_map/translate/pallas_call | solution.py:328
  125.3 1.8 %copy.9 = bf16[456,512]{1,0:T(8,128)(2,1)} copy(bf16[456,512]{1,0:T(8,128)(2,1)} %translate.1) | data formatting | bytes 933888

commit v2 on v1

--- a/solution.py
+++ b/solution.py
@@ -11,38 +11,66 @@
 LANES = 512
 NT = (((1,), (1,)), ((), ()))
 MESH = pl.DeviceIdType.MESH
-AHEAD = 3
+HALF = 256
+ROW, TILE = 5, 3
+AHEAD = 4
 LATE = 1
-
-
-def pick_rows(index_of, table_ref, picked_ref, unroll):
+ORDER = (
+    (0, 0), (1, 0), (2, 0), (0, 2), (0, 1), (3, 0), (1, 1), (2, 2),
+    (1, 2), (2, 1), (0, 3), (3, 1), (1, 3), (2, 3), (3, 2), (3, 3),
+)
+SHARED = {(0, 1), (0, 2), (0, 3), (1, 0), (1, 2), (1, 3), (2, 0), (2, 2), (3, 0), (3, 2)}
+
+
+def packed(digits, width):
+    total = sum(d << (width * i) for i, d in enumerate(digits))
+    return total - (1 << 32) if total >= 1 << 31 else total
+
+
+FIRST = packed([q[0] for q in ORDER], 2)
+SECOND = packed([q[1] for q in ORDER], 2)
+SHARES = packed([(n % 4, n // 4) in SHARED for n in range(16)], 1)
+
+
+def digit(code, place, width):
+    return lax.shift_right_logical(jnp.int32(code), width * place) & (2**width - 1)
+
+
+def node(step):
+    step = jnp.clip(step, 0, 15)
+    return digit(FIRST, step, 2), digit(SECOND, step, 2)
+
+
+def shared(q1, q2):
+    return digit(SHARES, q1 + 4 * q2, 1) == 1
+
+
+def pick_rows(index_of, table_ref, picked_ref, unroll, first=0, count=BOX):
     def chunk(i, carry):
         for u in range(64):
-            place = pl.multiple_of(i * 256 + (u // 8) * 32, 32) + u % 8
-            picked_ref[pl.ds(place, 4, stride=8), :] = table_ref[index_of(i * 64 + u)]
+            row = table_ref[index_of(i * 64 + u)]
+            picked_ref[pl.ds(i * (64 * ROW) + u * ROW, 4, stride=TILE), :] = row
         return carry
-    lax.fori_loop(0, BOX // 64, chunk, 0, unroll=unroll)
+    lax.fori_loop(first // 64, (first + count) // 64, chunk, 0, unroll=unroll)
 
 
 def spread_rows(picked_ref, table_ref, first):
     def chunk(i, carry):
         for u in range(64):
-            place = pl.multiple_of(i * 256 + (u // 8) * 32, 32) + u % 8
-            table_ref[first + i * 64 + u] = picked_ref[pl.ds(place, 4, stride=8), :]
+            place = pl.ds(i * (64 * ROW) + u * ROW, 4, stride=TILE)
+            table_ref[first + i * 64 + u] = picked_ref[place, :]
         return carry
     lax.fori_loop(0, BOX // 64, chunk, 0)
 
 
-def picked_value(picked_ref):
-    tiles = picked_ref[...].reshape(BOX // 8, 4, 8, 128)
-    return jnp.concatenate(
-        [tiles[:, c].reshape(BOX, 128) for c in range(4)], axis=1
-    ).astype(jnp.bfloat16)
+def picked_value(picked_ref, first=0, count=BOX):
+    tiles = [picked_ref[pl.ds(ROW * first + TILE * c, count, stride=ROW), :] for c in range(4)]
+    return jnp.concatenate(tiles, axis=1).astype(jnp.bfloat16)
 
 
 def set_picked(picked_ref, rows):
-    tiles = [rows[:, c * 128 : (c + 1) * 128].reshape(BOX // 8, 8, 128) for c in range(4)]
-    picked_ref[...] = jnp.stack(tiles, axis=1).reshape(BOX * 4, 128)
+    for c in range(4):
+        picked_ref[pl.ds(TILE * c, BOX, stride=ROW), :] = rows[:, c * 128 : (c + 1) * 128]
 
 
 def pad_lanes(rows):
@@ -50,16 +78,17 @@
 
 
 def kernel(
-    multipole_ref, send_list_ref, slot_hbm, ops_hbm, l2l_hbm, coarse_ref, out_ref,
-    slot_ref, ops_ref, l2l_ref, table_ref, even_ref, odd_ref, acc_ref, ghost_out, ghost_in,
+    multipole_ref, send_list_ref, source_ref, ops_hbm, l2l_hbm, coarse_ref, out_ref,
+    slot_vmem, slot_ref, ops_ref, l2l_ref, table_ref, even_ref, odd_ref, acc_ref, ghost_out, ghost_in,
     coarse_out, coarse_in, level_one, level_two,
     local_sem, op_send, op_recv, ghost_send, ghost_recv, coarse_send, coarse_recv,
 ):
     a, b = lax.axis_index("slab"), lax.axis_index("sub")
     z, y, x, core = a // 4, a % 4, b // 2, b % 2
 
+    slot_vmem[...] = source_ref[...] + 1
     local = [
-        pltpu.make_async_copy(slot_hbm, slot_ref, local_sem.at[0]),
+        pltpu.make_async_copy(slot_vmem, slot_ref, local_sem.at[0]),
         pltpu.make_async_copy(l2l_hbm, l2l_ref, local_sem.at[1]),
         pltpu.make_async_copy(ops_hbm, ops_ref.at[pl.ds(4 * a, 4)], local_sem.at[2]),
     ]
@@ -88,17 +117,6 @@
 
             greeted = greeted + here.astype(jnp.int32)
 
-    own = jnp.concatenate(
-        [multipole_ref[...].astype(jnp.float32), jnp.zeros((LANES - COEF, BOX), jnp.float32)], axis=0
-    ).T
-    set_picked(even_ref, own)
-    table_ref[0] = jnp.zeros((4, 128), jnp.float32)
-    spread_rows(even_ref, table_ref, 1)
-    coarse = jnp.concatenate(
-        [coarse_ref[...].astype(jnp.float32), jnp.zeros((LANES - COEF, 128), jnp.float32)], axis=0
-    ).T
-    coarse_out[...] = coarse[:16]
-
     pl.semaphore_wait(barrier, greeted)
 
     def source(cls, carrier, q1, q2):
@@ -111,11 +129,17 @@
 
     sign = 1 - 2 * core
 
+    def half(cls, y0, z0):
+        return (x + y0 + z0 + cls) % 2 == 0
+
     def links(cls, q1, q2, own_op):
         y0, z0, k = source(cls, core, q1, q2)
-        half = (x + y0 + z0 + cls) % 2 == 0
+        fed = half(cls, y0, z0)
         number = k // 4 * 2 + cls
         src = ops_hbm.at[2 * core + cls] if own_op else ops_ref.at[k]
+
+        def goes(p1, p2):
+            return fed | jnp.logical_not(shared(p1, p2))
 
         def copy(kind, device):
             return pltpu.make_async_remote_copy(
@@ -129,17 +153,18 @@
             return (4 * nz + ny, b)
 
         prim_y = cls == 0
-        back = along(~prim_y, -sign)
         beside = (a, ((x + sign + 4) % 4) * 2 + core)
+        ahead = ((q1 == 0) & goes(1, 0)) | ((q1 == 1) & goes(3, 0))
         kinds = [
-            ((q2 == 0) & (q1 <= 1), lambda: copy(0, along(prim_y, sign))),
-            ((q2 == 0) & (q1 == 0), lambda: copy(1, along(prim_y, -sign))),
-            ((q2 == 0) | ((q2 == 1) & half), lambda: copy(2, along(~prim_y, sign))),
+            ((q2 == 0) & ahead, lambda: copy(0, along(prim_y, sign))),
+            ((q2 == 0) & (q1 == 0) & goes(2, 0), lambda: copy(1, along(prim_y, -sign))),
             (
-                ((q2 == 0) | (q2 >= 2)) & half,
-                lambda: copy(3, (jnp.where(q2 == 0, back[0], a), jnp.where(q2 == 0, b, beside[1]))),
+                ((q2 == 0) & goes(q1, 1)) | ((q2 == 1) & goes(q1, 3)),
+                lambda: copy(2, along(~prim_y, sign)),
             ),
-            (q1 + q2 > 0, lambda: copy(4, (a, b + sign))),
+            ((q2 == 0) & goes(q1, 2), lambda: copy(3, along(~prim_y, -sign))),
+            (shared(q1, q2) & fed, lambda: copy(4, beside)),
+            (q1 + q2 > 0, lambda: copy(5, (a, b + sign))),
         ]
         return k, kinds
 
@@ -153,11 +178,12 @@
                 found[kind][1]().start()
 
     def over_x(cls, step):
-        y0, z0, _ = source(cls, core, step % 4, step // 4)
-        return (step >= 8) & ((x + y0 + z0 + cls) % 2 == 1)
+        q1, q2 = node(step)
+        y0, z0, _ = source(cls, core, q1, q2)
+        return shared(q1, q2) & jnp.logical_not(half(cls, y0, z0))
 
     def forward(cls, step):
-        k, found = links(cls, step % 4, step // 4, False)
+        k, found = links(cls, *node(step), False)
         pltpu.make_async_copy(ops_ref.at[k], ops_ref.at[k], op_recv.at[k]).wait()
         for condition, copy in found:
             @pl.when(condition)
@@ -166,6 +192,14 @@
 
     start_own(0, (0, 1))
     start_own(1, (0, 1))
+
+    own = jnp.concatenate(
+        [multipole_ref[...].astype(jnp.float32), jnp.zeros((LANES - COEF, BOX), jnp.float32)], axis=0
+    ).T
+    set_picked(even_ref, own)
+    table_ref[0] = jnp.zeros((4, 128), jnp.float32)
+    spread_rows(even_ref, table_ref, 1)
+    coarse_out[...] = pad_lanes(coarse_ref[...].astype(jnp.float32))
 
     has_coarse = b == a // 2
 
@@ -218,21 +252,28 @@
         for c in range(4):
             level_two[c, pl.ds(o, 8, stride=8), :] = children[:, c * 128 : (c + 1) * 128]
 
-    def apply(weight, picked_ref):
-        acc_ref[...] += lax.dot_general(
-            weight, picked_value(picked_ref)[:, :COEF], NT, preferred_element_type=jnp.float32
+    def apply(weight, picked_ref, first=0, count=BOX):
+        acc_ref[:, first : first + count] += lax.dot_general(
+            weight, picked_value(picked_ref, first, count)[:, :COEF], NT,
+            preferred_element_type=jnp.float32,
         )
 
     acc_ref[...] = jnp.zeros_like(acc_ref)
     even_ref[...] = jnp.zeros_like(even_ref)
 
     def octant(o, carry):
+        early = (o - 8) // 2 + AHEAD
+
+        @pl.when((early > 0) & jnp.logical_not(over_x(o % 2, early)))
+        def _():
+            forward(o % 2, early)
+
         for c in range(4):
             rounded = level_two[c].astype(jnp.bfloat16).astype(jnp.float32)
-            even_ref[pl.ds(c * 8 + o, BOX // 8, stride=32), :] = rounded
+            even_ref[pl.ds(ROW * o + TILE * c, BOX // 8, stride=8 * ROW), :] = rounded
         apply(l2l_ref[o], even_ref)
         for c in range(4):
-            even_ref[pl.ds(c * 8 + o, BOX // 8, stride=32), :] = jnp.zeros((BOX // 8, 128), jnp.float32)
+            even_ref[pl.ds(ROW * o + TILE * c, BOX // 8, stride=8 * ROW), :] = jnp.zeros((BOX // 8, 128), jnp.float32)
         return carry
 
     lax.fori_loop(0, 8, octant, 0)
@@ -247,19 +288,20 @@
 
     local[0].wait()
     local[2].wait()
-    for step in range(1, AHEAD):
-        forward(jnp.int32(0), jnp.int32(step))
-        forward(jnp.int32(1), jnp.int32(step))
-
     def op_pair(i):
         step, carrier = i // 2, (core + i) % 2
         return (
-            source(jnp.int32(0), carrier, step % 4, step // 4)[2],
-            source(jnp.int32(1), carrier, step % 4, step // 4)[2],
+            source(jnp.int32(0), carrier, *node(step))[2],
+            source(jnp.int32(1), carrier, *node(step))[2],
         )
 
-    def pick(k, picked_ref, unroll=True):
-        pick_rows(lambda t: slot_ref[k, t] + 1, table_ref, picked_ref, unroll)
+    def pick(k, picked_ref, unroll=True, first=0, count=BOX):
+        pick_rows(lambda t: slot_ref[k, t], table_ref, picked_ref, unroll, first, count)
+
+    def both(k_pick, pick_ref, k_apply, apply_ref):
+        for first in range(0, BOX, HALF):
+            pick(k_pick, pick_ref, True, first, HALF)
+            apply(ops_ref[k_apply], apply_ref, first, HALF)
 
     pick(op_pair(jnp.int32(0))[0], even_ref, False)
 
@@ -282,10 +324,8 @@
             for k in (k_even, k_odd):
                 pltpu.make_async_copy(ops_ref.at[k], ops_ref.at[k], op_recv.at[k]).wait()
 
-        pick(k_odd, odd_ref)
-        apply(ops_ref[k_even], even_ref)
-        pick(k_next, even_ref)
-        apply(ops_ref[k_odd], odd_ref)
+        both(k_odd, odd_ref, k_even, even_ref)
+        both(k_next, even_ref, k_odd, odd_ref)
         return carry
 
     lax.fori_loop(0, 32, main, 0)
@@ -293,14 +333,14 @@
 
     for cls in (0, 1):
         _, found = links(jnp.int32(cls), zero, zero, True)
-        for kind in range(4):
+        for kind in range(5):
             @pl.when(found[kind][0])
             def _():
                 found[kind][1]().wait_send()
 
     def drain(i, carry):
         step = i // 2
-        _, found = links(i % 2, step % 4, step // 4, False)
+        _, found = links(i % 2, *node(step), False)
         for condition, copy in found:
             @pl.when(condition)
             def _():
@@ -320,7 +360,6 @@
 
 
 def shards(multipole, send_list, source_slot, m2l_ops, l2l_ops, coarse_exp):
-    coarse = jnp.pad(coarse_exp, ((0, 0), (0, 112)))
     vmem = pl.BlockSpec(memory_space=pltpu.VMEM)
     smem = pl.BlockSpec(memory_space=pltpu.SMEM)
     hbm = pl.BlockSpec(memory_space=pltpu.HBM)
@@ -328,15 +367,16 @@
     return pl.pallas_call(
         kernel,
         out_shape=jax.ShapeDtypeStruct((COEF, BOX), bf16),
-        in_specs=[vmem, smem, hbm, hbm, hbm, vmem],
+        in_specs=[vmem, smem, vmem, hbm, hbm, vmem],
         out_specs=vmem,
         scratch_shapes=[
+            pltpu.VMEM((OFFSETS, BOX), jnp.int32),
             pltpu.SMEM((OFFSETS, BOX), jnp.int32),
             pltpu.VMEM((OFFSETS, COEF, COEF), bf16),
             pltpu.VMEM((8, COEF, COEF), bf16),
             pltpu.VMEM((COLS + 8, 4, 128), f32),
-            pltpu.VMEM((BOX * 4, 128), f32),
-            pltpu.VMEM((BOX * 4, 128), f32),
+            pltpu.VMEM((BOX * ROW + 16, 128), f32),
+            pltpu.VMEM((BOX * ROW + 16, 128), f32),
             pltpu.VMEM((COEF, BOX), f32),
             pltpu.VMEM((8, CAP, LANES), bf16),
             pltpu.VMEM((8, CAP, LANES), bf16),
@@ -345,7 +385,7 @@
             pltpu.VMEM((8, LANES), f32),
             pltpu.VMEM((4, 64, 128), f32),
             pltpu.SemaphoreType.DMA((3,)),
-            pltpu.SemaphoreType.DMA((5, 32)),
+            pltpu.SemaphoreType.DMA((6, 32)),
             pltpu.SemaphoreType.DMA((OFFSETS,)),
             pltpu.SemaphoreType.DMA((8,)),
             pltpu.SemaphoreType.DMA((8,)),
@@ -356,7 +396,7 @@
             collective_id=0, has_side_effects=True, vmem_limit_bytes=60 * 2**20
         ),
         name="translate",
-    )(multipole, send_list, source_slot, m2l_ops, l2l_ops, coarse)
+    )(multipole, send_list, source_slot, m2l_ops, l2l_ops, coarse_exp.T)
 
 
 def solution(mesh):

time: 129 us -> 113 us (0.88)
  the two profiles are of different devices: /device:TPU:1 before, /device:TPU:4 now
where the time goes in v2:
time: 113 us
  Pallas kernels  111 us (98%)
  local copies, waits for them, and re-layouts  1.82 us (2%)
    pallas_call x1, Pallas kernels, shards(): pl.pallas_call(kernel, out_shape=jax.ShapeDtypeStruct((COEF, BOX), bf16),...  111 us

profile of v2, /device:TPU:4, one launch (start us, length us, event | category | flops | bytes accessed | tf_op | source)
XLA Modules:
  0.0 113.3 jit_solution(3945647265400878028)
XLA Ops:
  0.0 111.5 %translate.1 = bf16[456,512]{1,0:T(8,128)(2,1)} custom-call(bf16[456,512]{1,0:T(8,128)(2,1)} %multipole_ref.1, s32[1,8,128]{2,1,0:T(8,128)} %send_list_ref.1, s32[64,512]{1,0:T(8,128)} %source_ref.1, bf16[4,456,456]{2,1,0:T(8,128)(2,1)} %ops_hbm.1, bf16[8,456,456]{2,1,0:T(8,128)(2,1)} %l2l_hbm.1, bf16[16,456]{1,0:T(8,128)(2,1)} %bitcast.1), custom_call_target="tpu_custom_call" | custom-call | tf_op jit(solution)/shard_map/translate/pallas_call | solution.py:367
  111.5 1.8 %copy.8 = bf16[456,512]{1,0:T(8,128)(2,1)} copy(bf16[456,512]{1,0:T(8,128)(2,1)} %translate.1) | data formatting | bytes 933888

commit v3 on v2

--- a/solution.py
+++ b/solution.py
@@ -45,20 +45,20 @@
     return digit(SHARES, q1 + 4 * q2, 1) == 1
 
 
-def pick_rows(index_of, table_ref, picked_ref, unroll, first=0, count=BOX):
+def pick_rows(place_ref, table_ref, picked_ref, first=0, count=BOX):
     def chunk(i, carry):
         for u in range(64):
-            row = table_ref[index_of(i * 64 + u)]
+            row = table_ref[pl.ds(place_ref[i * 64 + u], 4), :]
             picked_ref[pl.ds(i * (64 * ROW) + u * ROW, 4, stride=TILE), :] = row
         return carry
-    lax.fori_loop(first // 64, (first + count) // 64, chunk, 0, unroll=unroll)
+    lax.fori_loop(first // 64, (first + count) // 64, chunk, 0, unroll=True)
 
 
 def spread_rows(picked_ref, table_ref, first):
     def chunk(i, carry):
         for u in range(64):
             place = pl.ds(i * (64 * ROW) + u * ROW, 4, stride=TILE)
-            table_ref[first + i * 64 + u] = picked_ref[place, :]
+            table_ref[pl.ds(first * 4 + i * 256 + u * 4, 4), :] = picked_ref[place, :]
         return carry
     lax.fori_loop(0, BOX // 64, chunk, 0)
 
@@ -79,18 +79,23 @@
 
 def kernel(
     multipole_ref, send_list_ref, source_ref, ops_hbm, l2l_hbm, coarse_ref, out_ref,
-    slot_vmem, slot_ref, ops_ref, l2l_ref, table_ref, even_ref, odd_ref, acc_ref, ghost_out, ghost_in,
+    source_place, send_place, place_refs, ghost_places, ops_ref, l2l_ref, table_ref, even_ref, odd_ref, acc_ref, ghost_out, ghost_in,
     coarse_out, coarse_in, level_one, level_two,
-    local_sem, op_send, op_recv, ghost_send, ghost_recv, coarse_send, coarse_recv,
+    local_sem, place_sem, ghost_place_sem, op_send, op_recv, ghost_send, ghost_recv, coarse_send, coarse_recv,
 ):
     a, b = lax.axis_index("slab"), lax.axis_index("sub")
-    z, y, x, core = a // 4, a % 4, b // 2, b % 2
-
-    slot_vmem[...] = source_ref[...] + 1
+    z, y, x, core = a >> 2, a & 3, b >> 1, b & 1
+
+    source_place[...] = (source_ref[...] + 1) * 4
+    send_place[...] = (jnp.maximum(send_list_ref[0], 0) + 1) * 4
     local = [
-        pltpu.make_async_copy(slot_vmem, slot_ref, local_sem.at[0]),
-        pltpu.make_async_copy(l2l_hbm, l2l_ref, local_sem.at[1]),
-        pltpu.make_async_copy(ops_hbm, ops_ref.at[pl.ds(4 * a, 4)], local_sem.at[2]),
+        pltpu.make_async_copy(l2l_hbm, l2l_ref, local_sem.at[0]),
+        pltpu.make_async_copy(ops_hbm, ops_ref.at[pl.ds(4 * a, 4)], local_sem.at[1]),
+    ] + [
+        pltpu.make_async_copy(
+            send_place.at[n], ghost_places[n // 4].at[pl.ds(n % 4 * CAP, CAP)], ghost_place_sem.at[n]
+        )
+        for n in range(8)
     ]
     for copy in local:
         copy.start()
@@ -121,21 +126,21 @@
 
     def source(cls, carrier, q1, q2):
         sign = 1 - 2 * carrier
-        first = (q1 + (q1 == 2).astype(jnp.int32) - (q1 == 3).astype(jnp.int32)) * sign
-        second = (q2 + (q2 == 2).astype(jnp.int32) - (q2 == 3).astype(jnp.int32)) * sign
-        y0 = (y - jnp.where(cls == 0, first, second) + 4) % 4
-        z0 = (z - jnp.where(cls == 0, second, first) + 4) % 4
-        return y0, z0, 4 * (4 * z0 + y0) + 2 * carrier + cls
+        first = (q1 ^ (q1 >> 1)) * sign
+        second = (q2 ^ (q2 >> 1)) * sign
+        y0 = (y - jnp.where(cls == 0, first, second)) & 3
+        z0 = (z - jnp.where(cls == 0, second, first)) & 3
+        return y0, z0, 16 * z0 + 4 * y0 + 2 * carrier + cls
 
     sign = 1 - 2 * core
 
     def half(cls, y0, z0):
-        return (x + y0 + z0 + cls) % 2 == 0
+        return (x + y0 + z0 + cls) & 1 == 0
 
     def links(cls, q1, q2, own_op):
         y0, z0, k = source(cls, core, q1, q2)
         fed = half(cls, y0, z0)
-        number = k // 4 * 2 + cls
+        number = (k >> 2) * 2 + cls
         src = ops_hbm.at[2 * core + cls] if own_op else ops_ref.at[k]
 
         def goes(p1, p2):
@@ -148,12 +153,12 @@
             )
 
         def along(axis_is_y, by):
-            ny = jnp.where(axis_is_y, (y + by + 4) % 4, y)
-            nz = jnp.where(axis_is_y, z, (z + by + 4) % 4)
+            ny = jnp.where(axis_is_y, (y + by) & 3, y)
+            nz = jnp.where(axis_is_y, z, (z + by) & 3)
             return (4 * nz + ny, b)
 
         prim_y = cls == 0
-        beside = (a, ((x + sign + 4) % 4) * 2 + core)
+        beside = (a, ((x + sign) & 3) * 2 + core)
         ahead = ((q1 == 0) & goes(1, 0)) | ((q1 == 1) & goes(3, 0))
         kinds = [
             ((q2 == 0) & ahead, lambda: copy(0, along(prim_y, sign))),
@@ -197,7 +202,7 @@
         [multipole_ref[...].astype(jnp.float32), jnp.zeros((LANES - COEF, BOX), jnp.float32)], axis=0
     ).T
     set_picked(even_ref, own)
-    table_ref[0] = jnp.zeros((4, 128), jnp.float32)
+    table_ref[0:4, :] = jnp.zeros((4, 128), jnp.float32)
     spread_rows(even_ref, table_ref, 1)
     coarse_out[...] = pad_lanes(coarse_ref[...].astype(jnp.float32))
 
@@ -223,11 +228,10 @@
             recv_sem=ghost_recv.at[n], device_id=(a + da, b + db), device_id_type=MESH,
         )
 
+    for copy in local[2:]:
+        copy.wait()
     for part in range(2):
-        pick_rows(
-            lambda t: jnp.maximum(send_list_ref[0, 4 * part + t // CAP, t % CAP], 0) + 1,
-            table_ref, odd_ref, False,
-        )
+        pick_rows(ghost_places[part], table_ref, odd_ref)
         ghost_out[4 * part : 4 * part + 4] = picked_value(odd_ref).reshape(4, CAP, LANES)
         for n in range(4 * part, 4 * part + 4):
             @pl.when(exists(DIR_SLAB[n], DIR_SUB[n]))
@@ -240,7 +244,7 @@
     @pl.when(jnp.logical_not(has_coarse))
     def _():
         coarse_copy(1).wait_recv()
-    local[1].wait()
+    local[0].wait()
 
     parent = jnp.broadcast_to(coarse_in[pl.ds(b, 1), :], (8, LANES))[:, :COEF].astype(jnp.bfloat16)
     for o in range(8):
@@ -286,49 +290,81 @@
         set_picked(odd_ref, ghost_in[4 * part : 4 * part + 4].reshape(BOX, LANES).astype(jnp.float32))
         spread_rows(odd_ref, table_ref, 1 + BOX + part * BOX)
 
-    local[0].wait()
-    local[2].wait()
-    def op_pair(i):
-        step, carrier = i // 2, (core + i) % 2
-        return (
-            source(jnp.int32(0), carrier, *node(step))[2],
-            source(jnp.int32(1), carrier, *node(step))[2],
-        )
-
-    def pick(k, picked_ref, unroll=True, first=0, count=BOX):
-        pick_rows(lambda t: slot_ref[k, t], table_ref, picked_ref, unroll, first, count)
-
-    def both(k_pick, pick_ref, k_apply, apply_ref):
+    local[1].wait()
+
+    def ops_of(step):
+        return [
+            source(jnp.int32(cls), carrier, *node(step))[2]
+            for carrier in (core, 1 - core) for cls in (0, 1)
+        ]
+
+    def place_copy(k, n):
+        return pltpu.make_async_copy(source_place.at[k], place_refs[n], place_sem.at[n])
+
+    def both(n_pick, pick_ref, k_apply, apply_ref):
         for first in range(0, BOX, HALF):
-            pick(k_pick, pick_ref, True, first, HALF)
+            pick_rows(place_refs[n_pick], table_ref, pick_ref, first, HALF)
             apply(ops_ref[k_apply], apply_ref, first, HALF)
 
-    pick(op_pair(jnp.int32(0))[0], even_ref, False)
-
-    def main(i, carry):
-        early, late = i // 2 + AHEAD, i // 2 + LATE
-
-        @pl.when((early < 16) & jnp.logical_not(over_x(i % 2, early)))
-        def _():
-            forward(i % 2, early)
-
-        @pl.when((late < 16) & over_x(i % 2, late))
-        def _():
-            forward(i % 2, late)
-
-        k_even, k_odd = op_pair(i)
-        k_next = op_pair(jnp.minimum(i + 1, 31))[0]
-
-        @pl.when((i % 2 == 1) & (i > 1))
-        def _():
-            for k in (k_even, k_odd):
+    first_ops = ops_of(jnp.int32(0))
+    for n in range(4):
+        place_copy(first_ops[n], n).start()
+    place_copy(first_ops[0], 0).wait()
+    pick_rows(place_refs[0], table_ref, even_ref)
+    place_copy(ops_of(jnp.int32(1))[0], 0).start()
+
+    def main(step, carry):
+        early, late = step + AHEAD, step + LATE
+
+        def hand_on(cls):
+            @pl.when((early < 16) & jnp.logical_not(over_x(cls, early)))
+            def _():
+                forward(cls, early)
+
+            @pl.when((late < 16) & over_x(cls, late))
+            def _():
+                forward(cls, late)
+
+        now, then = ops_of(step), ops_of(step + 1)
+        after = ops_of(step + 2)
+        hand_on(jnp.int32(0))
+        place_copy(now[1], 1).wait()
+        both(1, odd_ref, now[0], even_ref)
+
+        @pl.when(step < 15)
+        def _():
+            place_copy(then[1], 1).start()
+
+        hand_on(jnp.int32(1))
+        place_copy(now[2], 2).wait()
+        both(2, even_ref, now[1], odd_ref)
+
+        @pl.when(step < 15)
+        def _():
+            place_copy(then[2], 2).start()
+
+        @pl.when(step > 0)
+        def _():
+            for k in now[2:]:
                 pltpu.make_async_copy(ops_ref.at[k], ops_ref.at[k], op_recv.at[k]).wait()
 
-        both(k_odd, odd_ref, k_even, even_ref)
-        both(k_next, even_ref, k_odd, odd_ref)
+        place_copy(now[3], 3).wait()
+        both(3, odd_ref, now[2], even_ref)
+
+        @pl.when(step < 15)
+        def _():
+            place_copy(then[3], 3).start()
+            place_copy(then[0], 0).wait()
+
+        both(0, even_ref, now[3], odd_ref)
+
+        @pl.when(step < 14)
+        def _():
+            place_copy(after[0], 0).start()
+
         return carry
 
-    lax.fori_loop(0, 32, main, 0)
+    lax.fori_loop(0, 16, main, 0)
     out_ref[...] = acc_ref[...].astype(out_ref.dtype)
 
     for cls in (0, 1):
@@ -361,20 +397,21 @@
 
 def shards(multipole, send_list, source_slot, m2l_ops, l2l_ops, coarse_exp):
     vmem = pl.BlockSpec(memory_space=pltpu.VMEM)
-    smem = pl.BlockSpec(memory_space=pltpu.SMEM)
     hbm = pl.BlockSpec(memory_space=pltpu.HBM)
     f32, bf16 = jnp.float32, jnp.bfloat16
     return pl.pallas_call(
         kernel,
         out_shape=jax.ShapeDtypeStruct((COEF, BOX), bf16),
-        in_specs=[vmem, smem, vmem, hbm, hbm, vmem],
+        in_specs=[vmem, vmem, vmem, hbm, hbm, vmem],
         out_specs=vmem,
         scratch_shapes=[
             pltpu.VMEM((OFFSETS, BOX), jnp.int32),
-            pltpu.SMEM((OFFSETS, BOX), jnp.int32),
+            pltpu.VMEM((8, CAP), jnp.int32),
+            [pltpu.SMEM((BOX,), jnp.int32)] * 4,
+            [pltpu.SMEM((BOX,), jnp.int32)] * 2,
             pltpu.VMEM((OFFSETS, COEF, COEF), bf16),
             pltpu.VMEM((8, COEF, COEF), bf16),
-            pltpu.VMEM((COLS + 8, 4, 128), f32),
+            pltpu.VMEM((4 * COLS + 32, 128), f32),
             pltpu.VMEM((BOX * ROW + 16, 128), f32),
             pltpu.VMEM((BOX * ROW + 16, 128), f32),
             pltpu.VMEM((COEF, BOX), f32),
@@ -384,7 +421,9 @@
             pltpu.VMEM((8, LANES), f32),
             pltpu.VMEM((8, LANES), f32),
             pltpu.VMEM((4, 64, 128), f32),
-            pltpu.SemaphoreType.DMA((3,)),
+            pltpu.SemaphoreType.DMA((2,)),
+            pltpu.SemaphoreType.DMA((4,)),
+            pltpu.SemaphoreType.DMA((8,)),
             pltpu.SemaphoreType.DMA((6, 32)),
             pltpu.SemaphoreType.DMA((OFFSETS,)),
             pltpu.SemaphoreType.DMA((8,)),

time: 113 us -> 91.5 us (0.81)
  the two profiles are of different devices: /device:TPU:4 before, /device:TPU:1 now
where the time goes in v3:
time: 91.5 us; the launch traced here: 91.4 us
  Pallas kernels  89.5 us (98%)
  local copies, waits for them, and re-layouts  1.82 us (2%)
    pallas_call x1, Pallas kernels, shards(): pl.pallas_call(kernel, out_shape=jax.ShapeDtypeStruct((COEF, BOX), bf16),...  89.5 us

profile of v3, /device:TPU:1, one launch (start us, length us, event | category | flops | bytes accessed | tf_op | source)
XLA Modules:
  0.0 91.4 jit_solution(17649861719362649768)
XLA Ops:
  0.0 89.5 %translate.1 = bf16[456,512]{1,0:T(8,128)(2,1)} custom-call(bf16[456,512]{1,0:T(8,128)(2,1)} %multipole_ref.1, s32[1,8,128]{2,1,0:T(8,128)} %send_list_ref.1, s32[64,512]{1,0:T(8,128)} %source_ref.1, bf16[4,456,456]{2,1,0:T(8,128)(2,1)} %ops_hbm.1, bf16[8,456,456]{2,1,0:T(8,128)(2,1)} %l2l_hbm.1, bf16[16,456]{1,0:T(8,128)(2,1)} %bitcast.1), custom_call_target="tpu_custom_call" | custom-call | tf_op jit(solution)/shard_map/translate/pallas_call | solution.py:402
  89.5 1.8 %copy.8 = bf16[456,512]{1,0:T(8,128)(2,1)} copy(bf16[456,512]{1,0:T(8,128)(2,1)} %translate.1) | data formatting | bytes 933888

commit v4 on v3

--- a/solution.py
+++ b/solution.py
@@ -13,7 +13,8 @@
 MESH = pl.DeviceIdType.MESH
 HALF = 256
 ROW, TILE = 5, 3
-AHEAD = 4
+AHEAD = 3
+PARTS = ((0, 256), (256, COEF - 256))
 LATE = 1
 ORDER = (
     (0, 0), (1, 0), (2, 0), (0, 2), (0, 1), (3, 0), (1, 1), (2, 2),
@@ -128,36 +129,36 @@
         sign = 1 - 2 * carrier
         first = (q1 ^ (q1 >> 1)) * sign
         second = (q2 ^ (q2 >> 1)) * sign
-        y0 = (y - jnp.where(cls == 0, first, second)) & 3
-        z0 = (z - jnp.where(cls == 0, second, first)) & 3
-        return y0, z0, 16 * z0 + 4 * y0 + 2 * carrier + cls
+        y0 = (y - (second if cls & 1 else first)) & 3
+        z0 = (z - (first if cls & 1 else second)) & 3
+        return y0, z0, 16 * z0 + 4 * y0 + 2 * carrier + (cls & 1)
 
     sign = 1 - 2 * core
 
     def half(cls, y0, z0):
-        return (x + y0 + z0 + cls) & 1 == 0
+        return (x + y0 + z0 + cls + (cls >> 1)) & 1 == 0
 
     def links(cls, q1, q2, own_op):
         y0, z0, k = source(cls, core, q1, q2)
         fed = half(cls, y0, z0)
-        number = (k >> 2) * 2 + cls
-        src = ops_hbm.at[2 * core + cls] if own_op else ops_ref.at[k]
+        number = (k >> 2) * 4 + cls
+        lanes = pl.ds(*PARTS[cls >> 1])
+        dst = ops_ref.at[k, :, lanes]
+        src = ops_hbm.at[2 * core + (cls & 1), :, lanes] if own_op else dst
 
         def goes(p1, p2):
             return fed | jnp.logical_not(shared(p1, p2))
 
         def copy(kind, device):
             return pltpu.make_async_remote_copy(
-                src_ref=src, dst_ref=ops_ref.at[k], send_sem=op_send.at[kind, number],
-                recv_sem=op_recv.at[k], device_id=device, device_id_type=MESH,
+                src_ref=src, dst_ref=dst, send_sem=op_send.at[kind, number],
+                recv_sem=op_recv.at[cls >> 1, k], device_id=device, device_id_type=MESH,
             )
 
         def along(axis_is_y, by):
-            ny = jnp.where(axis_is_y, (y + by) & 3, y)
-            nz = jnp.where(axis_is_y, z, (z + by) & 3)
-            return (4 * nz + ny, b)
-
-        prim_y = cls == 0
+            return (4 * z + ((y + by) & 3), b) if axis_is_y else (4 * ((z + by) & 3) + y, b)
+
+        prim_y = cls & 1 == 0
         beside = (a, ((x + sign) & 3) * 2 + core)
         ahead = ((q1 == 0) & goes(1, 0)) | ((q1 == 1) & goes(3, 0))
         kinds = [
@@ -165,9 +166,9 @@
             ((q2 == 0) & (q1 == 0) & goes(2, 0), lambda: copy(1, along(prim_y, -sign))),
             (
                 ((q2 == 0) & goes(q1, 1)) | ((q2 == 1) & goes(q1, 3)),
-                lambda: copy(2, along(~prim_y, sign)),
+                lambda: copy(2, along(not prim_y, sign)),
             ),
-            ((q2 == 0) & goes(q1, 2), lambda: copy(3, along(~prim_y, -sign))),
+            ((q2 == 0) & goes(q1, 2), lambda: copy(3, along(not prim_y, -sign))),
             (shared(q1, q2) & fed, lambda: copy(4, beside)),
             (q1 + q2 > 0, lambda: copy(5, (a, b + sign))),
         ]
@@ -176,7 +177,7 @@
     zero = jnp.int32(0)
 
     def start_own(cls, kinds):
-        _, found = links(jnp.int32(cls), zero, zero, True)
+        _, found = links(cls, zero, zero, True)
         for kind in kinds:
             @pl.when(found[kind][0])
             def _():
@@ -187,16 +188,20 @@
         y0, z0, _ = source(cls, core, q1, q2)
         return shared(q1, q2) & jnp.logical_not(half(cls, y0, z0))
 
+    def arrive(k, part):
+        here = ops_ref.at[k, :, pl.ds(*PARTS[part])]
+        pltpu.make_async_copy(here, here, op_recv.at[part, k]).wait()
+
     def forward(cls, step):
         k, found = links(cls, *node(step), False)
-        pltpu.make_async_copy(ops_ref.at[k], ops_ref.at[k], op_recv.at[k]).wait()
+        arrive(k, cls >> 1)
         for condition, copy in found:
             @pl.when(condition)
             def _():
                 copy().start()
 
-    start_own(0, (0, 1))
-    start_own(1, (0, 1))
+    for cls in range(4):
+        start_own(cls, (0, 1))
 
     own = jnp.concatenate(
         [multipole_ref[...].astype(jnp.float32), jnp.zeros((LANES - COEF, BOX), jnp.float32)], axis=0
@@ -238,8 +243,8 @@
             def _():
                 ghost_copy(n).start()
 
-    start_own(0, (2, 3))
-    start_own(1, (2, 3))
+    for cls in range(4):
+        start_own(cls, (2, 3))
 
     @pl.when(jnp.logical_not(has_coarse))
     def _():
@@ -265,22 +270,32 @@
     acc_ref[...] = jnp.zeros_like(acc_ref)
     even_ref[...] = jnp.zeros_like(even_ref)
 
-    def octant(o, carry):
-        early = (o - 8) // 2 + AHEAD
-
-        @pl.when((early > 0) & jnp.logical_not(over_x(o % 2, early)))
-        def _():
-            forward(o % 2, early)
-
-        for c in range(4):
-            rounded = level_two[c].astype(jnp.bfloat16).astype(jnp.float32)
-            even_ref[pl.ds(ROW * o + TILE * c, BOX // 8, stride=8 * ROW), :] = rounded
-        apply(l2l_ref[o], even_ref)
-        for c in range(4):
-            even_ref[pl.ds(ROW * o + TILE * c, BOX // 8, stride=8 * ROW), :] = jnp.zeros((BOX // 8, 128), jnp.float32)
+    def hand_on(cls, step):
+        early, late = step + AHEAD, step + LATE
+
+        @pl.when((early < 16) & jnp.logical_not(over_x(cls, early)))
+        def _():
+            forward(cls, early)
+
+        @pl.when((late > 0) & (late < 16) & over_x(cls, late))
+        def _():
+            forward(cls, late)
+
+    def octants(i, carry):
+        for cls in range(4):
+            o = 4 * i + cls
+            hand_on(cls, i - 2)
+            for c in range(4):
+                rounded = level_two[c].astype(jnp.bfloat16).astype(jnp.float32)
+                even_ref[pl.ds(ROW * o + TILE * c, BOX // 8, stride=8 * ROW), :] = rounded
+            apply(l2l_ref[o], even_ref)
+            for c in range(4):
+                even_ref[pl.ds(ROW * o + TILE * c, BOX // 8, stride=8 * ROW), :] = jnp.zeros(
+                    (BOX // 8, 128), jnp.float32
+                )
         return carry
 
-    lax.fori_loop(0, 8, octant, 0)
+    lax.fori_loop(0, 2, octants, 0)
 
     for part in range(2):
         for n in range(4 * part, 4 * part + 4):
@@ -294,7 +309,7 @@
 
     def ops_of(step):
         return [
-            source(jnp.int32(cls), carrier, *node(step))[2]
+            source(cls, carrier, *node(step))[2]
             for carrier in (core, 1 - core) for cls in (0, 1)
         ]
 
@@ -314,20 +329,9 @@
     place_copy(ops_of(jnp.int32(1))[0], 0).start()
 
     def main(step, carry):
-        early, late = step + AHEAD, step + LATE
-
-        def hand_on(cls):
-            @pl.when((early < 16) & jnp.logical_not(over_x(cls, early)))
-            def _():
-                forward(cls, early)
-
-            @pl.when((late < 16) & over_x(cls, late))
-            def _():
-                forward(cls, late)
-
         now, then = ops_of(step), ops_of(step + 1)
         after = ops_of(step + 2)
-        hand_on(jnp.int32(0))
+        hand_on(0, step)
         place_copy(now[1], 1).wait()
         both(1, odd_ref, now[0], even_ref)
 
@@ -335,7 +339,7 @@
         def _():
             place_copy(then[1], 1).start()
 
-        hand_on(jnp.int32(1))
+        hand_on(1, step)
         place_copy(now[2], 2).wait()
         both(2, even_ref, now[1], odd_ref)
 
@@ -343,10 +347,13 @@
         def _():
             place_copy(then[2], 2).start()
 
+        hand_on(2, step)
+
         @pl.when(step > 0)
         def _():
             for k in now[2:]:
-                pltpu.make_async_copy(ops_ref.at[k], ops_ref.at[k], op_recv.at[k]).wait()
+                arrive(k, 0)
+                arrive(k, 1)
 
         place_copy(now[3], 3).wait()
         both(3, odd_ref, now[2], even_ref)
@@ -356,6 +363,7 @@
             place_copy(then[3], 3).start()
             place_copy(then[0], 0).wait()
 
+        hand_on(3, step)
         both(0, even_ref, now[3], odd_ref)
 
         @pl.when(step < 14)
@@ -367,23 +375,23 @@
     lax.fori_loop(0, 16, main, 0)
     out_ref[...] = acc_ref[...].astype(out_ref.dtype)
 
-    for cls in (0, 1):
-        _, found = links(jnp.int32(cls), zero, zero, True)
+    for cls in range(4):
+        _, found = links(cls, zero, zero, True)
         for kind in range(5):
             @pl.when(found[kind][0])
             def _():
                 found[kind][1]().wait_send()
 
-    def drain(i, carry):
-        step = i // 2
-        _, found = links(i % 2, *node(step), False)
-        for condition, copy in found:
-            @pl.when(condition)
-            def _():
-                copy().wait_send()
+    def drain(step, carry):
+        for cls in range(4):
+            _, found = links(cls, *node(step), False)
+            for condition, copy in found:
+                @pl.when(condition)
+                def _():
+                    copy().wait_send()
         return carry
 
-    lax.fori_loop(2, 32, drain, 0)
+    lax.fori_loop(1, 16, drain, 0)
     for n in range(8):
         @pl.when(exists(DIR_SLAB[n], DIR_SUB[n]))
         def _():
@@ -424,8 +432,8 @@
             pltpu.SemaphoreType.DMA((2,)),
             pltpu.SemaphoreType.DMA((4,)),
             pltpu.SemaphoreType.DMA((8,)),
-            pltpu.SemaphoreType.DMA((6, 32)),
-            pltpu.SemaphoreType.DMA((OFFSETS,)),
+            pltpu.SemaphoreType.DMA((6, 64)),
+            pltpu.SemaphoreType.DMA((2, OFFSETS)),
             pltpu.SemaphoreType.DMA((8,)),
             pltpu.SemaphoreType.DMA((8,)),
             pltpu.SemaphoreType.DMA((7,)),

time: 91.5 us -> 95.3 us (1.042)
  Pallas kernels: 89.5 us -> 93.1 us
    pallas_call x1, Pallas kernels: 89.5 us -> 93.1 us  [shards(): pl.pallas_call(kernel, out_shape=jax.ShapeDtypeStruct((COEF, BOX), bf16),...]
where the time goes in v4:
time: 95.3 us; the launch traced here: 94.9 us
  Pallas kernels  93.1 us (98%)
  local copies, waits for them, and re-layouts  1.82 us (2%)
    pallas_call x1, Pallas kernels, shards(): pl.pallas_call(kernel, out_shape=jax.ShapeDtypeStruct((COEF, BOX), bf16),...  93.1 us

profile of v4, /device:TPU:1, one launch (start us, length us, event | category | flops | bytes accessed | tf_op | source)
XLA Modules:
  0.0 94.9 jit_solution(12734385907417117913)
XLA Ops:
  0.0 93.1 %translate.1 = bf16[456,512]{1,0:T(8,128)(2,1)} custom-call(bf16[456,512]{1,0:T(8,128)(2,1)} %multipole_ref.1, s32[1,8,128]{2,1,0:T(8,128)} %send_list_ref.1, s32[64,512]{1,0:T(8,128)} %source_ref.1, bf16[4,456,456]{2,1,0:T(8,128)(2,1)} %ops_hbm.1, bf16[8,456,456]{2,1,0:T(8,128)(2,1)} %l2l_hbm.1, bf16[16,456]{1,0:T(8,128)(2,1)} %bitcast.1), custom_call_target="tpu_custom_call" | custom-call | tf_op jit(solution)/shard_map/translate/pallas_call | solution.py:410
  93.1 1.8 %copy.8 = bf16[456,512]{1,0:T(8,128)(2,1)} copy(bf16[456,512]{1,0:T(8,128)(2,1)} %translate.1) | data formatting | bytes 933888

commit v5 on v4

--- a/solution.py
+++ b/solution.py
@@ -14,7 +14,7 @@
 HALF = 256
 ROW, TILE = 5, 3
 AHEAD = 3
-PARTS = ((0, 256), (256, COEF - 256))
+PARTS = ((0, 224), (224, COEF - 224))
 LATE = 1
 ORDER = (
     (0, 0), (1, 0), (2, 0), (0, 2), (0, 1), (3, 0), (1, 1), (2, 2),
@@ -142,9 +142,9 @@
         y0, z0, k = source(cls, core, q1, q2)
         fed = half(cls, y0, z0)
         number = (k >> 2) * 4 + cls
-        lanes = pl.ds(*PARTS[cls >> 1])
-        dst = ops_ref.at[k, :, lanes]
-        src = ops_hbm.at[2 * core + (cls & 1), :, lanes] if own_op else dst
+        rows = pl.ds(*PARTS[cls >> 1])
+        dst = ops_ref.at[k, rows]
+        src = ops_hbm.at[2 * core + (cls & 1), rows] if own_op else dst
 
         def goes(p1, p2):
             return fed | jnp.logical_not(shared(p1, p2))
@@ -189,7 +189,7 @@
         return shared(q1, q2) & jnp.logical_not(half(cls, y0, z0))
 
     def arrive(k, part):
-        here = ops_ref.at[k, :, pl.ds(*PARTS[part])]
+        here = ops_ref.at[k, pl.ds(*PARTS[part])]
         pltpu.make_async_copy(here, here, op_recv.at[part, k]).wait()
 
     def forward(cls, step):

time: 95.3 us -> 95.1 us (level)
  no operation moved by 1% of the time
where the time goes in v5:
time: 95.1 us; the launch traced here: 94.6 us
  Pallas kernels  92.8 us (98%)
  local copies, waits for them, and re-layouts  1.82 us (2%)
    pallas_call x1, Pallas kernels, shards(): pl.pallas_call(kernel, out_shape=jax.ShapeDtypeStruct((COEF, BOX), bf16),...  92.8 us

profile of v5, /device:TPU:1, one launch (start us, length us, event | category | flops | bytes accessed | tf_op | source)
XLA Modules:
  0.0 94.6 jit_solution(17445682821933272534)
XLA Ops:
  0.0 92.8 %translate.1 = bf16[456,512]{1,0:T(8,128)(2,1)} custom-call(bf16[456,512]{1,0:T(8,128)(2,1)} %multipole_ref.1, s32[1,8,128]{2,1,0:T(8,128)} %send_list_ref.1, s32[64,512]{1,0:T(8,128)} %source_ref.1, bf16[4,456,456]{2,1,0:T(8,128)(2,1)} %ops_hbm.1, bf16[8,456,456]{2,1,0:T(8,128)(2,1)} %l2l_hbm.1, bf16[16,456]{1,0:T(8,128)(2,1)} %bitcast.1), custom_call_target="tpu_custom_call" | custom-call | tf_op jit(solution)/shard_map/translate/pallas_call | solution.py:410
  92.8 1.8 %copy.8 = bf16[456,512]{1,0:T(8,128)(2,1)} copy(bf16[456,512]{1,0:T(8,128)(2,1)} %translate.1) | data formatting | bytes 933888

commit v6 on v3

--- a/solution.py
+++ b/solution.py
@@ -16,10 +16,10 @@
 AHEAD = 4
 LATE = 1
 ORDER = (
-    (0, 0), (1, 0), (2, 0), (0, 2), (0, 1), (3, 0), (1, 1), (2, 2),
-    (1, 2), (2, 1), (0, 3), (3, 1), (1, 3), (2, 3), (3, 2), (3, 3),
+    (0, 0), (1, 0), (2, 0), (0, 2), (0, 1), (3, 0), (1, 2), (1, 1),
+    (0, 3), (2, 2), (2, 1), (3, 1), (3, 2), (1, 3), (2, 3), (3, 3),
 )
-SHARED = {(0, 1), (0, 2), (0, 3), (1, 0), (1, 2), (1, 3), (2, 0), (2, 2), (3, 0), (3, 2)}
+SHARED = {(0, 1), (0, 2), (0, 3), (1, 2), (1, 3), (2, 0), (2, 2), (3, 0), (3, 2)}
 
 
 def packed(digits, width):

time: 91.5 us -> 95.9 us (1.048)
  the two profiles are of different devices: /device:TPU:1 before, /device:TPU:32 now
where the time goes in v6:
time: 95.9 us; the launch traced here: 95.7 us
  Pallas kernels  93.9 us (98%)
  local copies, waits for them, and re-layouts  1.82 us (2%)
    pallas_call x1, Pallas kernels, shards(): pl.pallas_call(kernel, out_shape=jax.ShapeDtypeStruct((COEF, BOX), bf16),...  93.9 us

profile of v6, /device:TPU:32, one launch (start us, length us, event | category | flops | bytes accessed | tf_op | source)
XLA Modules:
  0.0 95.7 jit_solution(15545154954514176744)
XLA Ops:
  0.0 93.9 %translate.1 = bf16[456,512]{1,0:T(8,128)(2,1)} custom-call(bf16[456,512]{1,0:T(8,128)(2,1)} %multipole_ref.1, s32[1,8,128]{2,1,0:T(8,128)} %send_list_ref.1, s32[64,512]{1,0:T(8,128)} %source_ref.1, bf16[4,456,456]{2,1,0:T(8,128)(2,1)} %ops_hbm.1, bf16[8,456,456]{2,1,0:T(8,128)(2,1)} %l2l_hbm.1, bf16[16,456]{1,0:T(8,128)(2,1)} %bitcast.1), custom_call_target="tpu_custom_call" | custom-call | tf_op jit(solution)/shard_map/translate/pallas_call | solution.py:402
  93.9 1.8 %copy.8 = bf16[456,512]{1,0:T(8,128)(2,1)} copy(bf16[456,512]{1,0:T(8,128)(2,1)} %translate.1) | data formatting | bytes 933888

commit v7 on v3

--- a/solution.py
+++ b/solution.py
@@ -14,6 +14,7 @@
 HALF = 256
 ROW, TILE = 5, 3
 AHEAD = 4
+SENT = 60
 LATE = 1
 ORDER = (
     (0, 0), (1, 0), (2, 0), (0, 2), (0, 1), (3, 0), (1, 1), (2, 2),
@@ -85,6 +86,28 @@
 ):
     a, b = lax.axis_index("slab"), lax.axis_index("sub")
     z, y, x, core = a >> 2, a & 3, b >> 1, b & 1
+
+    def exists(da, db):
+        row, col = a + da, b + db
+        return (row >= 0) & (row < 16) & (col >= 0) & (col < 8)
+
+    ghost_in[...] = jnp.zeros_like(ghost_in)
+    barrier = pltpu.get_barrier_semaphore()
+    for step in range(1, 8):
+        pl.semaphore_signal(barrier, inc=1, device_id=(a, (b + step) % 8), device_id_type=MESH)
+    for dy, dz in ((1, 0), (3, 0), (0, 1), (0, 3)):
+        there = ((z + dz) % 4) * 4 + (y + dy) % 4
+        pl.semaphore_signal(barrier, inc=1, device_id=(there, b), device_id_type=MESH)
+    greeted = 11
+    for da, db in zip(DIR_SLAB, DIR_SUB):
+        if da != 0:
+            here = exists(da, db)
+
+            @pl.when(here)
+            def _():
+                pl.semaphore_signal(barrier, inc=1, device_id=(a + da, b + db), device_id_type=MESH)
+
+            greeted = greeted + here.astype(jnp.int32)
 
     source_place[...] = (source_ref[...] + 1) * 4
     send_place[...] = (jnp.maximum(send_list_ref[0], 0) + 1) * 4
@@ -100,28 +123,6 @@
     for copy in local:
         copy.start()
 
-    def exists(da, db):
-        row, col = a + da, b + db
-        return (row >= 0) & (row < 16) & (col >= 0) & (col < 8)
-
-    ghost_in[...] = jnp.zeros_like(ghost_in)
-    barrier = pltpu.get_barrier_semaphore()
-    for step in range(1, 8):
-        pl.semaphore_signal(barrier, inc=1, device_id=(a, (b + step) % 8), device_id_type=MESH)
-    for dy, dz in ((1, 0), (3, 0), (0, 1), (0, 3)):
-        there = ((z + dz) % 4) * 4 + (y + dy) % 4
-        pl.semaphore_signal(barrier, inc=1, device_id=(there, b), device_id_type=MESH)
-    greeted = 11
-    for da, db in zip(DIR_SLAB, DIR_SUB):
-        if da != 0:
-            here = exists(da, db)
-
-            @pl.when(here)
-            def _():
-                pl.semaphore_signal(barrier, inc=1, device_id=(a + da, b + db), device_id_type=MESH)
-
-            greeted = greeted + here.astype(jnp.int32)
-
     pl.semaphore_wait(barrier, greeted)
 
     def source(cls, carrier, q1, q2):
@@ -140,15 +141,14 @@
     def links(cls, q1, q2, own_op):
         y0, z0, k = source(cls, core, q1, q2)
         fed = half(cls, y0, z0)
-        number = (k >> 2) * 2 + cls
         src = ops_hbm.at[2 * core + cls] if own_op else ops_ref.at[k]
 
         def goes(p1, p2):
             return fed | jnp.logical_not(shared(p1, p2))
 
-        def copy(kind, device):
+        def copy(device):
             return pltpu.make_async_remote_copy(
-                src_ref=src, dst_ref=ops_ref.at[k], send_sem=op_send.at[kind, number],
+                src_ref=src, dst_ref=ops_ref.at[k], send_sem=op_send,
                 recv_sem=op_recv.at[k], device_id=device, device_id_type=MESH,
             )
 
@@ -161,15 +161,15 @@
         beside = (a, ((x + sign) & 3) * 2 + core)
         ahead = ((q1 == 0) & goes(1, 0)) | ((q1 == 1) & goes(3, 0))
         kinds = [
-            ((q2 == 0) & ahead, lambda: copy(0, along(prim_y, sign))),
-            ((q2 == 0) & (q1 == 0) & goes(2, 0), lambda: copy(1, along(prim_y, -sign))),
+            ((q2 == 0) & ahead, lambda: copy(along(prim_y, sign))),
+            ((q2 == 0) & (q1 == 0) & goes(2, 0), lambda: copy(along(prim_y, -sign))),
             (
                 ((q2 == 0) & goes(q1, 1)) | ((q2 == 1) & goes(q1, 3)),
-                lambda: copy(2, along(~prim_y, sign)),
+                lambda: copy(along(~prim_y, sign)),
             ),
-            ((q2 == 0) & goes(q1, 2), lambda: copy(3, along(~prim_y, -sign))),
-            (shared(q1, q2) & fed, lambda: copy(4, beside)),
-            (q1 + q2 > 0, lambda: copy(5, (a, b + sign))),
+            ((q2 == 0) & goes(q1, 2), lambda: copy(along(~prim_y, -sign))),
+            (shared(q1, q2) & fed, lambda: copy(beside)),
+            (q1 + q2 > 0, lambda: copy((a, b + sign))),
         ]
         return k, kinds
 
@@ -367,23 +367,8 @@
     lax.fori_loop(0, 16, main, 0)
     out_ref[...] = acc_ref[...].astype(out_ref.dtype)
 
-    for cls in (0, 1):
-        _, found = links(jnp.int32(cls), zero, zero, True)
-        for kind in range(5):
-            @pl.when(found[kind][0])
-            def _():
-                found[kind][1]().wait_send()
-
-    def drain(i, carry):
-        step = i // 2
-        _, found = links(i % 2, *node(step), False)
-        for condition, copy in found:
-            @pl.when(condition)
-            def _():
-                copy().wait_send()
-        return carry
-
-    lax.fori_loop(2, 32, drain, 0)
+    sent = ops_ref.at[pl.ds(0, SENT)]
+    pltpu.make_async_copy(sent, sent, op_send).wait()
     for n in range(8):
         @pl.when(exists(DIR_SLAB[n], DIR_SUB[n]))
         def _():
@@ -424,7 +409,7 @@
             pltpu.SemaphoreType.DMA((2,)),
             pltpu.SemaphoreType.DMA((4,)),
             pltpu.SemaphoreType.DMA((8,)),
-            pltpu.SemaphoreType.DMA((6, 32)),
+            pltpu.SemaphoreType.DMA,
             pltpu.SemaphoreType.DMA((OFFSETS,)),
             pltpu.SemaphoreType.DMA((8,)),
             pltpu.SemaphoreType.DMA((8,)),

time: 91.5 us -> 88.6 us (0.968)
  Pallas kernels: 89.5 us -> 86.6 us
    pallas_call x1, Pallas kernels: 89.5 us -> 86.6 us  [shards(): pl.pallas_call(kernel, out_shape=jax.ShapeDtypeStruct((COEF, BOX), bf16),...]
where the time goes in v7:
time: 88.6 us; the launch traced here: 88.4 us
  Pallas kernels  86.6 us (98%)
  local copies, waits for them, and re-layouts  1.82 us (2%)
    pallas_call x1, Pallas kernels, shards(): pl.pallas_call(kernel, out_shape=jax.ShapeDtypeStruct((COEF, BOX), bf16),...  86.6 us
    unnamed x1, local copies, waits for them, and re-layouts  1.82 us

profile of v7, /device:TPU:1, one launch (start us, length us, event | category | flops | bytes accessed | tf_op | source)
XLA Modules:
  0.0 88.4 jit_solution(3389253986055039192)
XLA Ops:
  0.0 86.6 %translate.1 = bf16[456,512]{1,0:T(8,128)(2,1)} custom-call(bf16[456,512]{1,0:T(8,128)(2,1)} %multipole_ref.1, s32[1,8,128]{2,1,0:T(8,128)} %send_list_ref.1, s32[64,512]{1,0:T(8,128)} %source_ref.1, bf16[4,456,456]{2,1,0:T(8,128)(2,1)} %ops_hbm.1, bf16[8,456,456]{2,1,0:T(8,128)(2,1)} %l2l_hbm.1, bf16[16,456]{1,0:T(8,128)(2,1)} %bitcast.1), custom_call_target="tpu_custom_call" | custom-call | tf_op jit(solution)/shard_map/translate/pallas_call | solution.py:387
  86.6 1.8 %copy.8 = bf16[456,512]{1,0:T(8,128)(2,1)} copy(bf16[456,512]{1,0:T(8,128)(2,1)} %translate.1) | data formatting | bytes 933888

commit v8 on v7

--- a/solution.py
+++ b/solution.py
@@ -30,7 +30,29 @@
 
 FIRST = packed([q[0] for q in ORDER], 2)
 SECOND = packed([q[1] for q in ORDER], 2)
-SHARES = packed([(n % 4, n // 4) in SHARED for n in range(16)], 1)
+
+
+def children(q):
+    q1, q2 = q
+    return (
+        {(0, 0): (1, 0), (1, 0): (3, 0)}.get(q),
+        (2, 0) if q == (0, 0) else None,
+        {0: (q1, 1), 1: (q1, 3)}.get(q2),
+        (q1, 2) if q2 == 0 else None,
+    )
+
+
+def masks(kind):
+    found = [children(q)[kind] for q in ORDER]
+    return (
+        packed([n is not None and n not in SHARED for n in found], 1),
+        packed([n is not None for n in found], 1),
+    )
+
+
+KINDS = tuple(masks(kind) for kind in range(4))
+SHARES = packed([q in SHARED for q in ORDER], 1)
+TURNS = packed([(q[0] in (1, 2)) ^ (q[1] in (1, 2)) for q in ORDER], 1)
 
 
 def digit(code, place, width):
@@ -40,10 +62,6 @@
 def node(step):
     step = jnp.clip(step, 0, 15)
     return digit(FIRST, step, 2), digit(SECOND, step, 2)
-
-
-def shared(q1, q2):
-    return digit(SHARES, q1 + 4 * q2, 1) == 1
 
 
 def pick_rows(place_ref, table_ref, picked_ref, first=0, count=BOX):
@@ -135,16 +153,17 @@
 
     sign = 1 - 2 * core
 
-    def half(cls, y0, z0):
-        return (x + y0 + z0 + cls) & 1 == 0
-
-    def links(cls, q1, q2, own_op):
-        y0, z0, k = source(cls, core, q1, q2)
-        fed = half(cls, y0, z0)
+    def feeds(cls, step):
+        return (x + y + z + cls + digit(TURNS, step, 1)) & 1 == 0
+
+    def links(cls, step, own_op):
+        _, _, k = source(cls, core, *node(step))
+        fed = feeds(cls, step)
         src = ops_hbm.at[2 * core + cls] if own_op else ops_ref.at[k]
 
-        def goes(p1, p2):
-            return fed | jnp.logical_not(shared(p1, p2))
+        def goes(kind):
+            always, feeding = KINDS[kind]
+            return jnp.where(fed, digit(feeding, step, 1), digit(always, step, 1)) == 1
 
         def copy(device):
             return pltpu.make_async_remote_copy(
@@ -159,36 +178,32 @@
 
         prim_y = cls == 0
         beside = (a, ((x + sign) & 3) * 2 + core)
-        ahead = ((q1 == 0) & goes(1, 0)) | ((q1 == 1) & goes(3, 0))
         kinds = [
-            ((q2 == 0) & ahead, lambda: copy(along(prim_y, sign))),
-            ((q2 == 0) & (q1 == 0) & goes(2, 0), lambda: copy(along(prim_y, -sign))),
-            (
-                ((q2 == 0) & goes(q1, 1)) | ((q2 == 1) & goes(q1, 3)),
-                lambda: copy(along(~prim_y, sign)),
-            ),
-            ((q2 == 0) & goes(q1, 2), lambda: copy(along(~prim_y, -sign))),
-            (shared(q1, q2) & fed, lambda: copy(beside)),
-            (q1 + q2 > 0, lambda: copy((a, b + sign))),
+            (goes(0), lambda: copy(along(prim_y, sign))),
+            (goes(1), lambda: copy(along(prim_y, -sign))),
+            (goes(2), lambda: copy(along(~prim_y, sign))),
+            (goes(3), lambda: copy(along(~prim_y, -sign))),
+            (fed & (digit(SHARES, step, 1) == 1), lambda: copy(beside)),
+            (step > 0, lambda: copy((a, b + sign))),
         ]
         return k, kinds
 
     zero = jnp.int32(0)
 
     def start_own(cls, kinds):
-        _, found = links(jnp.int32(cls), zero, zero, True)
+        _, found = links(jnp.int32(cls), zero, True)
         for kind in kinds:
             @pl.when(found[kind][0])
             def _():
                 found[kind][1]().start()
 
     def over_x(cls, step):
-        q1, q2 = node(step)
-        y0, z0, _ = source(cls, core, q1, q2)
-        return shared(q1, q2) & jnp.logical_not(half(cls, y0, z0))
+        step = jnp.clip(step, 0, 15)
+        return (digit(SHARES, step, 1) == 1) & jnp.logical_not(feeds(cls, step))
 
     def forward(cls, step):
-        k, found = links(cls, *node(step), False)
+        step = jnp.clip(step, 0, 15)
+        k, found = links(cls, step, False)
         pltpu.make_async_copy(ops_ref.at[k], ops_ref.at[k], op_recv.at[k]).wait()
         for condition, copy in found:
             @pl.when(condition)

time: 88.6 us -> 88.4 us (level)
  no operation moved by 1% of the time
where the time goes in v8:
time: 88.4 us; the launch traced here: 88.2 us
  Pallas kernels  86.4 us (98%)
  local copies, waits for them, and re-layouts  1.82 us (2%)
    pallas_call x1, Pallas kernels, shards(): pl.pallas_call(kernel, out_shape=jax.ShapeDtypeStruct((COEF, BOX), bf16),...  86.4 us
    unnamed x1, local copies, waits for them, and re-layouts  1.82 us

profile of v8, /device:TPU:1, one launch (start us, length us, event | category | flops | bytes accessed | tf_op | source)
XLA Modules:
  0.0 88.2 jit_solution(17954598870267796357)
XLA Ops:
  0.0 86.4 %translate.1 = bf16[456,512]{1,0:T(8,128)(2,1)} custom-call(bf16[456,512]{1,0:T(8,128)(2,1)} %multipole_ref.1, s32[1,8,128]{2,1,0:T(8,128)} %send_list_ref.1, s32[64,512]{1,0:T(8,128)} %source_ref.1, bf16[4,456,456]{2,1,0:T(8,128)(2,1)} %ops_hbm.1, bf16[8,456,456]{2,1,0:T(8,128)(2,1)} %l2l_hbm.1, bf16[16,456]{1,0:T(8,128)(2,1)} %bitcast.1), custom_call_target="tpu_custom_call" | custom-call | tf_op jit(solution)/shard_map/translate/pallas_call | solution.py:402
  86.4 1.8 %copy.8 = bf16[456,512]{1,0:T(8,128)(2,1)} copy(bf16[456,512]{1,0:T(8,128)(2,1)} %translate.1) | data formatting | bytes 933888

commit v9 on v8

--- a/solution.py
+++ b/solution.py
@@ -13,7 +13,7 @@
 MESH = pl.DeviceIdType.MESH
 HALF = 256
 ROW, TILE = 5, 3
-AHEAD = 4
+AHEAD = 3
 SENT = 60
 LATE = 1
 ORDER = (

time: 88.4 us -> 93.8 us (1.061)
  the two profiles are of different devices: /device:TPU:1 before, /device:TPU:2 now
where the time goes in v9:
time: 93.8 us; the launch traced here: 93.6 us
  Pallas kernels  91.8 us (98%)
  local copies, waits for them, and re-layouts  1.82 us (2%)
    pallas_call x1, Pallas kernels, shards(): pl.pallas_call(kernel, out_shape=jax.ShapeDtypeStruct((COEF, BOX), bf16),...  91.8 us

profile of v9, /device:TPU:2, one launch (start us, length us, event | category | flops | bytes accessed | tf_op | source)
XLA Modules:
  0.0 93.6 jit_solution(3796256692450002954)
XLA Ops:
  0.0 91.8 %translate.1 = bf16[456,512]{1,0:T(8,128)(2,1)} custom-call(bf16[456,512]{1,0:T(8,128)(2,1)} %multipole_ref.1, s32[1,8,128]{2,1,0:T(8,128)} %send_list_ref.1, s32[64,512]{1,0:T(8,128)} %source_ref.1, bf16[4,456,456]{2,1,0:T(8,128)(2,1)} %ops_hbm.1, bf16[8,456,456]{2,1,0:T(8,128)(2,1)} %l2l_hbm.1, bf16[16,456]{1,0:T(8,128)(2,1)} %bitcast.1), custom_call_target="tpu_custom_call" | custom-call | tf_op jit(solution)/shard_map/translate/pallas_call | solution.py:402
  91.8 1.8 %copy.8 = bf16[456,512]{1,0:T(8,128)(2,1)} copy(bf16[456,512]{1,0:T(8,128)(2,1)} %translate.1) | data formatting | bytes 933888
